TPU v7x, 32 devices: a whole 2x2x4 slice. The times are simulated.
32 devices in a mesh: row: 8 (over z, y), col: 4 (over x, core).
Axes of the slice: x: 2, y: 2, z: 4, core: 2. Of those that a mesh axis runs over, the one named last changes fastest.
Arguments:
- feats: bfloat16 [64, 64, 128], P(('row', 'col')), may hold values from -6 to 6
- coords: bfloat16 [64, 3, 128], P(('row', 'col')), may hold values from 0 to 1
- valid: int32 [64, 128], P(('row', 'col')), may hold values 0 or 1
- pairs: int32 [8, 4, 8, 2], P('row', 'col'), may hold values from 0 to 15, as said below
- pair_count: int32 [8, 4], P('row', 'col'), may hold values from 1 to 8, as said below
- w_first: bfloat16 [128, 128], replicated, may hold values from -0.5 to 0.5
- bias_first: float32 [128], replicated, may hold values from -3 to 3
- dist_scale: float32 [128], replicated, may hold values from -3 to 3
- w_second: bfloat16 [64, 128], replicated, may hold values from -0.5 to 0.5
- bias_second: float32 [64], replicated, may hold values from -3 to 3
- cotangent: bfloat16 [64, 64, 128], P(('row', 'col')), may hold values from -6 to 6
Outputs:
- updated: bfloat16 [64, 64, 128], P(('row', 'col'))
- grad_feats: float32 [64, 64, 128], P(('row', 'col'))
- grad_first: float32 [128, 128], replicated
- grad_bias_first: float32 [128], replicated
- grad_dist: float32 [128], replicated
- grad_second: float32 [64, 128], replicated
- grad_bias_second: float32 [64], replicated
Inputs may be any that keep to these rules, and one draw needn't show every extreme that they name: pairs[r, c, p, 0] names a cell of row block r by its place, below 8; pairs[r, c, p, 1] a cell of column block c by its place, below 16. `pair_count`: some grid position has all 8 pairs live.
All inputs are finite; a program needn't handle non-finite values. No bound on the sum of `valid` on one device may be relied on, other than what follows from the above.
Results may differ from a plain program's by a relative error of at most 0.0045.
Values may be sent and summed in bfloat16 or wider, within the bound.
No kernel may reach another device: no remote copies, remote signals or barrier semaphores. Data moves between devices by JAX's collectives and lax.ppermute only.
A program may use at most 64 MiB of HBM per device.

v0:
```python
import jax
import jax.numpy as jnp
from jax import lax
from jax.sharding import PartitionSpec as P

L = 64
H = 128
CP = 128
TILE_GROUP = 1


def silu_slope(value):
    sigm = jax.nn.sigmoid(value)
    return sigm * (1.0 + value * (1.0 - sigm))


def tile_forward(
    proj_row,
    proj_col,
    pos_row,
    pos_col,
    mask_row,
    mask_col,
    w_second,
    bias_first,
    dist_scale,
    bias_second,
    active,
):
    offsets = pos_row[:, :, None] - pos_col[:, None, :]
    sq_dist = jnp.sum(offsets * offsets, axis=0)
    pre_hidden = (
        proj_row[:, :, None]
        + proj_col[:, None, :]
        + dist_scale[:, None, None] * sq_dist[None]
        + bias_first[:, None, None]
    )
    hidden = jax.nn.silu(pre_hidden).astype(jnp.bfloat16)
    pre_message = (
        jnp.einsum("mh,hij->mij", w_second, hidden, preferred_element_type=jnp.float32)
        + bias_second[:, None, None]
    )
    message = jax.nn.silu(pre_message)
    envelope = active * mask_row[:, None] * mask_col[None, :] / (1.0 + sq_dist) / CP
    gathered_msg = jnp.sum(envelope[None] * message, axis=2)
    return (gathered_msg, sq_dist, pre_hidden, hidden, pre_message, envelope)


def tile_terms(
    proj_row,
    proj_col,
    pos_row,
    pos_col,
    mask_row,
    mask_col,
    grad_row,
    w_second,
    bias_first,
    dist_scale,
    bias_second,
    active,
):
    gathered_msg, sq_dist, pre_hidden, hidden, pre_message, envelope = tile_forward(
        proj_row,
        proj_col,
        pos_row,
        pos_col,
        mask_row,
        mask_col,
        w_second,
        bias_first,
        dist_scale,
        bias_second,
        active,
    )
    grad_outer = envelope[None] * grad_row[:, :, None] * silu_slope(pre_message)
    grad_low = grad_outer.astype(jnp.bfloat16)
    grad_w2 = jnp.einsum("mij,hij->mh", grad_low, hidden, preferred_element_type=jnp.float32)
    grad_b2 = jnp.sum(grad_outer, axis=(1, 2))
    grad_hidden = jnp.einsum("mh,mij->hij", w_second, grad_low, preferred_element_type=jnp.float32)
    grad_inner = grad_hidden * silu_slope(pre_hidden)
    return (
        gathered_msg,
        jnp.sum(grad_inner, axis=2),
        jnp.sum(grad_inner, axis=1),
        grad_w2,
        grad_b2,
        jnp.sum(grad_inner * sq_dist[None], axis=(1, 2)),
        jnp.sum(grad_inner, axis=(1, 2)),
    )


def sweep(group_step, init, slots):
    groups = slots // TILE_GROUP
    return lax.fori_loop(0, groups, group_step, init)


def per_device(
    feats,
    coords,
    valid,
    pairs,
    pair_count,
    w_first,
    bias_first,
    dist_scale,
    w_second,
    bias_second,
    cotangent,
):
    tile_count = pair_count[0, 0]
    pair_list = pairs[0, 0]
    slots = pair_list.shape[0]
    mask_low = valid.astype(jnp.bfloat16)
    row_feats, row_coords, row_valid = (
        lax.all_gather(feats, "col", axis=0, tiled=True),
        lax.all_gather(coords, "col", axis=0, tiled=True),
        lax.all_gather(mask_low, "col", axis=0, tiled=True),
    )
    col_feats, col_coords, col_valid = (
        lax.all_gather(feats, "row", axis=0, tiled=True),
        lax.all_gather(coords, "row", axis=0, tiled=True),
        lax.all_gather(mask_low, "row", axis=0, tiled=True),
    )
    proj_row = jnp.einsum(
        "hl,clp->chp", w_first[:, :L], row_feats, preferred_element_type=jnp.float32
    )
    proj_col = jnp.einsum(
        "hl,clp->chp", w_first[:, L:], col_feats, preferred_element_type=jnp.float32
    )
    row_pos = row_coords.astype(jnp.float32)
    col_pos = col_coords.astype(jnp.float32)
    row_mask = row_valid.astype(jnp.float32)
    col_mask = col_valid.astype(jnp.float32)
    row_count = row_feats.shape[0]
    col_count = col_feats.shape[0]
    params = (w_second, bias_first, dist_scale, bias_second)

    def select(group):
        tiles = group * TILE_GROUP + jnp.arange(TILE_GROUP)
        active = (tiles < tile_count).astype(jnp.float32)
        return (pair_list[tiles, 0], pair_list[tiles, 1], active)

    batched_forward = jax.vmap(tile_forward, in_axes=(0, 0, 0, 0, 0, 0, None, None, None, None, 0))
    batched_terms = jax.vmap(tile_terms, in_axes=(0, 0, 0, 0, 0, 0, 0, None, None, None, None, 0))

    def forward_step(group, agg_state):
        row_cells, col_cells, active = select(group)
        pieces = batched_forward(
            proj_row[row_cells],
            proj_col[col_cells],
            row_pos[row_cells],
            col_pos[col_cells],
            row_mask[row_cells],
            col_mask[col_cells],
            *params,
            active
        )
        return agg_state.at[row_cells].add(pieces[0])

    agg_zero = jnp.zeros((row_count, L, CP), jnp.float32)
    agg_rows = sweep(forward_step, agg_zero, slots)
    own_agg = lax.psum_scatter(agg_rows, "col", scatter_dimension=0, tiled=True)
    row_cotan = lax.all_gather(cotangent, "col", axis=0, tiled=True)
    row_grad = row_cotan.astype(jnp.float32)

    def add_backward(state, terms, row_cells, col_cells):
        return (
            state[0].at[row_cells].add(terms[1]),
            state[1].at[col_cells].add(terms[2]),
            state[2] + jnp.sum(terms[3], axis=0),
            state[3] + jnp.sum(terms[4], axis=0),
            state[4] + jnp.sum(terms[5], axis=0),
            state[5] + jnp.sum(terms[6], axis=0),
        )

    def group_terms(group):
        row_cells, col_cells, active = select(group)
        terms = batched_terms(
            proj_row[row_cells],
            proj_col[col_cells],
            row_pos[row_cells],
            col_pos[col_cells],
            row_mask[row_cells],
            col_mask[col_cells],
            row_grad[row_cells],
            *params,
            active
        )
        return (terms, row_cells, col_cells)

    def backward_step(group, state):
        terms, row_cells, col_cells = group_terms(group)
        return add_backward(state, terms, row_cells, col_cells)

    back_zero = (
        jnp.zeros((row_count, H, CP), jnp.float32),
        jnp.zeros((col_count, H, CP), jnp.float32),
        jnp.zeros((L, H), jnp.float32),
        jnp.zeros((L,), jnp.float32),
        jnp.zeros((H,), jnp.float32),
        jnp.zeros((H,), jnp.float32),
    )
    grad_rows, grad_cols, grad_w2, grad_b2, grad_ds, grad_b1 = sweep(
        backward_step, back_zero, slots
    )
    w_rows = w_first[:, :L].astype(jnp.float32)
    w_cols = w_first[:, L:].astype(jnp.float32)
    row_feat_grad = jnp.einsum("hl,chp->clp", w_rows, grad_rows, precision=lax.Precision.HIGHEST)
    col_feat_grad = jnp.einsum("hl,chp->clp", w_cols, grad_cols, precision=lax.Precision.HIGHEST)
    own_rows = lax.psum_scatter(
        row_feat_grad.astype(jnp.bfloat16), "col", scatter_dimension=0, tiled=True
    ).astype(jnp.float32)
    own_cols = lax.psum_scatter(
        col_feat_grad.astype(jnp.bfloat16), "row", scatter_dimension=0, tiled=True
    ).astype(jnp.float32)
    local_first = jnp.concatenate(
        [
            jnp.einsum(
                "chp,clp->hl",
                grad_rows,
                row_feats.astype(jnp.float32),
                precision=lax.Precision.HIGHEST,
            ),
            jnp.einsum(
                "chp,clp->hl",
                grad_cols,
                col_feats.astype(jnp.float32),
                precision=lax.Precision.HIGHEST,
            ),
        ],
        axis=1,
    )
    grad_first, grad_b1, grad_ds, grad_w2, grad_b2 = lax.psum(
        (local_first, grad_b1, grad_ds, grad_w2, grad_b2), ("row", "col")
    )
    updated = (feats.astype(jnp.float32) + own_agg).astype(jnp.bfloat16)
    grad_feats = cotangent.astype(jnp.float32) + own_rows + own_cols
    return (updated, grad_feats, grad_first, grad_b1, grad_ds, grad_w2, grad_b2)


def solution(mesh):
    placed = (
        P(("row", "col"), None, None),
        P(("row", "col"), None, None),
        P(("row", "col"), None),
        P("row", "col", None, None),
        P("row", "col"),
        P(),
        P(),
        P(),
        P(),
        P(),
        P(("row", "col"), None, None),
    )
    return jax.shard_map(
        per_device,
        mesh=mesh,
        in_specs=placed,
        out_specs=(
            P(("row", "col"), None, None),
            P(("row", "col"), None, None),
            P(),
            P(),
            P(),
            P(),
            P(),
        ),
        check_vma=False,
    )
```

profile of v0, /device:TPU:0, one launch (start us, length us, event | category | flops | bytes accessed | tf_op | source)
XLA Modules:
  0.0 592.2 jit_solution(6262369693875292626)
XLA Ops:
  8.8 5.9 %all-gather = bf16[4,2,128]{2,1,0:T(2,128)(2,1)S(1)} all-gather(bf16[1,2,128]{2,1,0:T(2,128)(2,1)S(1)} %convert_bitcast_fusion), channel_id=1, replica_groups=mesh['row'=8,'col'=4] {'col'}, dimensions={0}, use_global_device_ids=true | all-gather | bytes 2560 | tf_op jit(solution)/shard_map/all_gather | solution.py:118
  14.7 21.2 %all-gather.1 = bf16[8,2,128]{2,1,0:T(2,128)(2,1)S(1)} all-gather(bf16[1,2,128]{2,1,0:T(2,128)(2,1)S(1)} %convert_bitcast_fusion), channel_id=1, replica_groups=mesh['row'=8,'col'=4] {'row'}, dimensions={0}, use_global_device_ids=true | all-gather | bytes 4608 | tf_op jit(solution)/shard_map/all_gather | solution.py:123
  36.6 5.1 all_gather.23
  41.8 26.0 %all_gather.24 = bf16[16,3,128]{2,1,0:T(4,128)(2,1)S(1)} all-gather(bf16[2,3,128]{2,1,0:T(4,128)(2,1)S(1)} %copy.43), channel_id=1, replica_groups=mesh['row'=8,'col'=4] {'row'}, dimensions={0}, use_global_device_ids=true | all-gather | bytes 13824 | tf_op jit(solution)/shard_map/all_gather | solution.py:122
  67.7 5.6 all_gather.25
  73.4 30.9 %all_gather.26 = bf16[16,64,128]{2,1,0:T(8,128)(2,1)S(1)} all-gather(bf16[2,64,128]{2,1,0:T(8,128)(2,1)} %param.21), channel_id=1, replica_groups=mesh['row'=8,'col'=4] {'row'}, dimensions={0}, use_global_device_ids=true | all-gather | bytes 294912 | tf_op jit(solution)/shard_map/all_gather | solution.py:121
  106.2 5.6 all_gather.27
  114.9 236.4 %while.58 = (s32[]{:T(128)}, f32[8,128,128]{1,2,0:T(8,128)S(1)}, f32[16,128,128]{1,2,0:T(8,128)S(1)}, f32[64,128]{1,0:T(8,128)}, f32[64]{0:T(128)}, /*index=5*/f...) while((s32[]{:T(128)}, f32[8,128,128]{1,2,0:T(8,128)S(1)}, ...), condition=%wide.region_15.16_spmd.clone, body=%wide.region_6.15_spmd.clone.sunk | while | flops 891535808 | bytes 8555537 | solution.py:95
  127.0 6.0 %fusion.93 = (f32[64]{0:T(128)S(1)}, bf16[64,128,128]{2,0,1:T(8,128)(2,1)S(1)}) fusion(f32[64]{0:T(128)} %get-tuple-element.1450, bf16[64,128]{1,0:T(8,128)(2,1)} %get-tuple-element.1449, f32[128]{0:T(128)} %get-tuple-element.1448, f32[128,128]{1,0:T(8,128)S(1)} %multiply_reduce_fusion.6, f32[128]{0:T(128)} %get-tuple-element.1447, ...), kind=kOutput, calls=%fused_computation.112.clone.1 | convolution fusion | flops 299892672 | bytes 2409984 | tf_op jit(solution)/shard_map/while/body/eval_jaxpr/vmap(mh,hij->mij)/dot_general | solution.py:40
  133.1 3.1 fusion.96
  136.3 6.9 %fusion.94 = (f32[128]{0:T(128)S(1)}, f32[128]{0:T(128)S(1)}, f32[128,128]{0,1:T(8,128)S(1)}, f32[128,128]{0,1:T(8,128)S(1)}) fusion(f32[128,128]{1,0:T(8,128)S(1)} %multiply_reduce_fusion.6, f32[128]{0:T(128)S(1)} %copy-done.22, f32[128]{0:T(128)S(1)} %copy-done.20, f32[128,128]{0,1:T(8,128)S(1)} %dynamic-slice_bitcast_fusion.7, ...), kind=kOutput, calls=%fused_computation.111.clone.1 | convolution fusion | flops 304054016 | bytes 2443264 | tf_op jit(solution)/shard_map/while/body/eval_jaxpr/vmap(mh,mij->hij)/dot_general | solution.py:80
  156.6 6.0 %fusion.93 = (f32[64]{0:T(128)S(1)}, bf16[64,128,128]{2,0,1:T(8,128)(2,1)S(1)}) fusion(f32[64]{0:T(128)} %get-tuple-element.1450, bf16[64,128]{1,0:T(8,128)(2,1)} %get-tuple-element.1449, f32[128]{0:T(128)} %get-tuple-element.1448, f32[128,128]{1,0:T(8,128)S(1)} %multiply_reduce_fusion.6, f32[128]{0:T(128)} %get-tuple-element.1447, ...), kind=kOutput, calls=%fused_computation.112.clone.1 | convolution fusion | flops 299892672 | bytes 2409984 | tf_op jit(solution)/shard_map/while/body/eval_jaxpr/vmap(mh,hij->mij)/dot_general | solution.py:40
  162.7 3.1 fusion.96
  165.8 6.9 %fusion.94 = (f32[128]{0:T(128)S(1)}, f32[128]{0:T(128)S(1)}, f32[128,128]{0,1:T(8,128)S(1)}, f32[128,128]{0,1:T(8,128)S(1)}) fusion(f32[128,128]{1,0:T(8,128)S(1)} %multiply_reduce_fusion.6, f32[128]{0:T(128)S(1)} %copy-done.22, f32[128]{0:T(128)S(1)} %copy-done.20, f32[128,128]{0,1:T(8,128)S(1)} %dynamic-slice_bitcast_fusion.7, ...), kind=kOutput, calls=%fused_computation.111.clone.1 | convolution fusion | flops 304054016 | bytes 2443264 | tf_op jit(solution)/shard_map/while/body/eval_jaxpr/vmap(mh,mij->hij)/dot_general | solution.py:80
  186.1 6.0 %fusion.93 = (f32[64]{0:T(128)S(1)}, bf16[64,128,128]{2,0,1:T(8,128)(2,1)S(1)}) fusion(f32[64]{0:T(128)} %get-tuple-element.1450, bf16[64,128]{1,0:T(8,128)(2,1)} %get-tuple-element.1449, f32[128]{0:T(128)} %get-tuple-element.1448, f32[128,128]{1,0:T(8,128)S(1)} %multiply_reduce_fusion.6, f32[128]{0:T(128)} %get-tuple-element.1447, ...), kind=kOutput, calls=%fused_computation.112.clone.1 | convolution fusion | flops 299892672 | bytes 2409984 | tf_op jit(solution)/shard_map/while/body/eval_jaxpr/vmap(mh,hij->mij)/dot_general | solution.py:40
  192.2 3.1 fusion.96
  195.4 6.9 %fusion.94 = (f32[128]{0:T(128)S(1)}, f32[128]{0:T(128)S(1)}, f32[128,128]{0,1:T(8,128)S(1)}, f32[128,128]{0,1:T(8,128)S(1)}) fusion(f32[128,128]{1,0:T(8,128)S(1)} %multiply_reduce_fusion.6, f32[128]{0:T(128)S(1)} %copy-done.22, f32[128]{0:T(128)S(1)} %copy-done.20, f32[128,128]{0,1:T(8,128)S(1)} %dynamic-slice_bitcast_fusion.7, ...), kind=kOutput, calls=%fused_computation.111.clone.1 | convolution fusion | flops 304054016 | bytes 2443264 | tf_op jit(solution)/shard_map/while/body/eval_jaxpr/vmap(mh,mij->hij)/dot_general | solution.py:80
  215.7 6.0 %fusion.93 = (f32[64]{0:T(128)S(1)}, bf16[64,128,128]{2,0,1:T(8,128)(2,1)S(1)}) fusion(f32[64]{0:T(128)} %get-tuple-element.1450, bf16[64,128]{1,0:T(8,128)(2,1)} %get-tuple-element.1449, f32[128]{0:T(128)} %get-tuple-element.1448, f32[128,128]{1,0:T(8,128)S(1)} %multiply_reduce_fusion.6, f32[128]{0:T(128)} %get-tuple-element.1447, ...), kind=kOutput, calls=%fused_computation.112.clone.1 | convolution fusion | flops 299892672 | bytes 2409984 | tf_op jit(solution)/shard_map/while/body/eval_jaxpr/vmap(mh,hij->mij)/dot_general | solution.py:40
  221.8 3.1 fusion.96
  224.9 6.9 %fusion.94 = (f32[128]{0:T(128)S(1)}, f32[128]{0:T(128)S(1)}, f32[128,128]{0,1:T(8,128)S(1)}, f32[128,128]{0,1:T(8,128)S(1)}) fusion(f32[128,128]{1,0:T(8,128)S(1)} %multiply_reduce_fusion.6, f32[128]{0:T(128)S(1)} %copy-done.22, f32[128]{0:T(128)S(1)} %copy-done.20, f32[128,128]{0,1:T(8,128)S(1)} %dynamic-slice_bitcast_fusion.7, ...), kind=kOutput, calls=%fused_computation.111.clone.1 | convolution fusion | flops 304054016 | bytes 2443264 | tf_op jit(solution)/shard_map/while/body/eval_jaxpr/vmap(mh,mij->hij)/dot_general | solution.py:80
  245.2 6.0 %fusion.93 = (f32[64]{0:T(128)S(1)}, bf16[64,128,128]{2,0,1:T(8,128)(2,1)S(1)}) fusion(f32[64]{0:T(128)} %get-tuple-element.1450, bf16[64,128]{1,0:T(8,128)(2,1)} %get-tuple-element.1449, f32[128]{0:T(128)} %get-tuple-element.1448, f32[128,128]{1,0:T(8,128)S(1)} %multiply_reduce_fusion.6, f32[128]{0:T(128)} %get-tuple-element.1447, ...), kind=kOutput, calls=%fused_computation.112.clone.1 | convolution fusion | flops 299892672 | bytes 2409984 | tf_op jit(solution)/shard_map/while/body/eval_jaxpr/vmap(mh,hij->mij)/dot_general | solution.py:40
  251.3 3.1 fusion.96
  254.5 6.9 %fusion.94 = (f32[128]{0:T(128)S(1)}, f32[128]{0:T(128)S(1)}, f32[128,128]{0,1:T(8,128)S(1)}, f32[128,128]{0,1:T(8,128)S(1)}) fusion(f32[128,128]{1,0:T(8,128)S(1)} %multiply_reduce_fusion.6, f32[128]{0:T(128)S(1)} %copy-done.22, f32[128]{0:T(128)S(1)} %copy-done.20, f32[128,128]{0,1:T(8,128)S(1)} %dynamic-slice_bitcast_fusion.7, ...), kind=kOutput, calls=%fused_computation.111.clone.1 | convolution fusion | flops 304054016 | bytes 2443264 | tf_op jit(solution)/shard_map/while/body/eval_jaxpr/vmap(mh,mij->hij)/dot_general | solution.py:80
  274.8 6.0 %fusion.93 = (f32[64]{0:T(128)S(1)}, bf16[64,128,128]{2,0,1:T(8,128)(2,1)S(1)}) fusion(f32[64]{0:T(128)} %get-tuple-element.1450, bf16[64,128]{1,0:T(8,128)(2,1)} %get-tuple-element.1449, f32[128]{0:T(128)} %get-tuple-element.1448, f32[128,128]{1,0:T(8,128)S(1)} %multiply_reduce_fusion.6, f32[128]{0:T(128)} %get-tuple-element.1447, ...), kind=kOutput, calls=%fused_computation.112.clone.1 | convolution fusion | flops 299892672 | bytes 2409984 | tf_op jit(solution)/shard_map/while/body/eval_jaxpr/vmap(mh,hij->mij)/dot_general | solution.py:40
  280.9 3.1 fusion.96
  284.0 6.9 %fusion.94 = (f32[128]{0:T(128)S(1)}, f32[128]{0:T(128)S(1)}, f32[128,128]{0,1:T(8,128)S(1)}, f32[128,128]{0,1:T(8,128)S(1)}) fusion(f32[128,128]{1,0:T(8,128)S(1)} %multiply_reduce_fusion.6, f32[128]{0:T(128)S(1)} %copy-done.22, f32[128]{0:T(128)S(1)} %copy-done.20, f32[128,128]{0,1:T(8,128)S(1)} %dynamic-slice_bitcast_fusion.7, ...), kind=kOutput, calls=%fused_computation.111.clone.1 | convolution fusion | flops 304054016 | bytes 2443264 | tf_op jit(solution)/shard_map/while/body/eval_jaxpr/vmap(mh,mij->hij)/dot_general | solution.py:80
  304.3 6.0 %fusion.93 = (f32[64]{0:T(128)S(1)}, bf16[64,128,128]{2,0,1:T(8,128)(2,1)S(1)}) fusion(f32[64]{0:T(128)} %get-tuple-element.1450, bf16[64,128]{1,0:T(8,128)(2,1)} %get-tuple-element.1449, f32[128]{0:T(128)} %get-tuple-element.1448, f32[128,128]{1,0:T(8,128)S(1)} %multiply_reduce_fusion.6, f32[128]{0:T(128)} %get-tuple-element.1447, ...), kind=kOutput, calls=%fused_computation.112.clone.1 | convolution fusion | flops 299892672 | bytes 2409984 | tf_op jit(solution)/shard_map/while/body/eval_jaxpr/vmap(mh,hij->mij)/dot_general | solution.py:40
  310.4 3.1 fusion.96
  313.6 6.9 %fusion.94 = (f32[128]{0:T(128)S(1)}, f32[128]{0:T(128)S(1)}, f32[128,128]{0,1:T(8,128)S(1)}, f32[128,128]{0,1:T(8,128)S(1)}) fusion(f32[128,128]{1,0:T(8,128)S(1)} %multiply_reduce_fusion.6, f32[128]{0:T(128)S(1)} %copy-done.22, f32[128]{0:T(128)S(1)} %copy-done.20, f32[128,128]{0,1:T(8,128)S(1)} %dynamic-slice_bitcast_fusion.7, ...), kind=kOutput, calls=%fused_computation.111.clone.1 | convolution fusion | flops 304054016 | bytes 2443264 | tf_op jit(solution)/shard_map/while/body/eval_jaxpr/vmap(mh,mij->hij)/dot_general | solution.py:80
  333.9 6.0 %fusion.93 = (f32[64]{0:T(128)S(1)}, bf16[64,128,128]{2,0,1:T(8,128)(2,1)S(1)}) fusion(f32[64]{0:T(128)} %get-tuple-element.1450, bf16[64,128]{1,0:T(8,128)(2,1)} %get-tuple-element.1449, f32[128]{0:T(128)} %get-tuple-element.1448, f32[128,128]{1,0:T(8,128)S(1)} %multiply_reduce_fusion.6, f32[128]{0:T(128)} %get-tuple-element.1447, ...), kind=kOutput, calls=%fused_computation.112.clone.1 | convolution fusion | flops 299892672 | bytes 2409984 | tf_op jit(solution)/shard_map/while/body/eval_jaxpr/vmap(mh,hij->mij)/dot_general | solution.py:40
  340.0 3.1 fusion.96
  343.1 6.9 %fusion.94 = (f32[128]{0:T(128)S(1)}, f32[128]{0:T(128)S(1)}, f32[128,128]{0,1:T(8,128)S(1)}, f32[128,128]{0,1:T(8,128)S(1)}) fusion(f32[128,128]{1,0:T(8,128)S(1)} %multiply_reduce_fusion.6, f32[128]{0:T(128)S(1)} %copy-done.22, f32[128]{0:T(128)S(1)} %copy-done.20, f32[128,128]{0,1:T(8,128)S(1)} %dynamic-slice_bitcast_fusion.7, ...), kind=kOutput, calls=%fused_computation.111.clone.1 | convolution fusion | flops 304054016 | bytes 2443264 | tf_op jit(solution)/shard_map/while/body/eval_jaxpr/vmap(mh,mij->hij)/dot_general | solution.py:80
  354.5 124.6 %while.57 = (s32[]{:T(128)}, f32[8,64,128]{2,1,0:T(8,128)}, s32[8,2]{0,1:T(2,128)S(1)}, s32[1,1]{1,0:T(1,128)}, f32[8,128]{1,0:T(8,128)}, /*index=5*/f32[16,128]...) while((s32[]{:T(128)}, f32[8,64,128]{2,1,0:T(8,128)}, ...), condition=%wide.region_4.5_spmd, body=%wide.region_0.4_spmd.sunk | while | flops 294854816 | bytes 1276019 | solution.py:95
  363.4 5.3 fusion.86
  375.0 1.4 and_reduce_fusion.6
  379.0 5.3 fusion.86
  390.6 1.4 and_reduce_fusion.6
  394.6 5.3 fusion.86
  410.1 5.3 fusion.86
  425.7 5.3 fusion.86
  441.3 5.3 fusion.86
  456.9 5.3 fusion.86
  472.5 5.3 fusion.86
  480.4 1.5 fusion.45
  482.0 37.7 %all-reduce = (f32[128]{0:T(128)}, f32[128]{0:T(128)}, f32[64,128]{1,0:T(8,128)}, f32[64]{0:T(128)}) all-reduce(f32[128]{0:T(128)S(1)} %copy-done.12, f32[128]{0:T(128)S(1)} %copy-done.15, f32[64,128]{1,0:T(8,128)S(1)} %copy-done.9, f32[64]{0:T(128)S(1)} %copy-done.18), channel_id=1, replica_groups=mesh['row'=8,'col'=4] {'row','col'}, use_global_device_ids=true, to_apply=%region_19.20 | all-reduce | flops 8512 | bytes 68096 | tf_op jit(solution)/shard_map/psum | solution.py:234
  519.7 1.6 copy.54
  521.3 1.5 add_convert_fusion
  522.7 60.5 %reduce-scatter.8.cloned.1.call-done = bf16[2,64,128]{2,1,0:T(8,128)(2,1)} async-done(((bf16[16,64,128]{2,1,0:T(8,128)(2,1)}), bf16[2,64,128]{2,1,0:T(8,128)(2,1)}) %reduce-scatter.8.cloned.1.call-update) | async-done | bytes 32784 | tf_op jit(solution)/shard_map/reduce_scatter | solution.py:214
  (474 shorter events, 129.5 us)
Async XLA Ops:
  8.0 511.7 %all-reduce.3.cloned.1.call-start = ((), (), s32[]{:S(2)}) async-start(), calls=%async_computation.6 | async-start | bytes 131072 | tf_op jit(solution)/shard_map/psum | solution.py:234
  73.4 39.2 %copy-start.2 = (bf16[8,64,128]{2,1,0:T(8,128)(2,1)}, bf16[8,64,128]{2,1,0:T(8,128)(2,1)S(1)}, u32[]{:S(2)}) copy-start(bf16[8,64,128]{2,1,0:T(8,128)(2,1)S(1)} %all_gather.25) | copy-start | bytes 393220
  104.3 10.4 %copy-start = (bf16[16,64,128]{2,1,0:T(8,128)(2,1)}, bf16[16,64,128]{2,1,0:T(8,128)(2,1)S(1)}, u32[]{:S(2)}) copy-start(bf16[16,64,128]{2,1,0:T(8,128)(2,1)S(1)} %all_gather.26) | copy-start | bytes 786436
  106.2 8.7 %copy-start.6 = (s32[1,1,8,2]{2,3,1,0:T(2,128)S(1)}, s32[1,1,8,2]{2,3,1,0:T(2,128)}, u32[]{:S(2)}) copy-start(s32[1,1,8,2]{2,3,1,0:T(2,128)} %param.24) | copy-start | bytes 196
  114.9 236.5 %copy-start.1 = (bf16[16,64,128]{2,1,0:T(8,128)(2,1)S(1)}, bf16[16,64,128]{2,1,0:T(8,128)(2,1)}, u32[]{:S(2)}) copy-start(bf16[16,64,128]{2,1,0:T(8,128)(2,1)} %copy-done) | copy-start | bytes 786436
  127.0 6.0 %copy-start.7 = (f32[64,128]{1,0:T(8,128)S(1)}, f32[64,128]{1,0:T(8,128)}, u32[]{:S(2)}) copy-start(f32[64,128]{1,0:T(8,128)} %get-tuple-element.1407) | copy-start | bytes 98308 | tf_op jit(solution)/shard_map/while
  127.0 6.0 %copy-start.20 = (f32[128]{0:T(128)S(1)}, f32[128]{0:T(128)}, u32[]{:S(2)}) copy-start(f32[128]{0:T(128)} %get-tuple-element.1447) | copy-start | bytes 1540 | tf_op jit(solution)/shard_map/while
  136.3 6.9 %copy-start.8 = (f32[64,128]{1,0:T(8,128)}, f32[64,128]{1,0:T(8,128)S(1)}, u32[]{:S(2)}) copy-start(f32[64,128]{1,0:T(8,128)S(1)} %fusion.96) | copy-start | bytes 98308 | tf_op jit(solution)/shard_map/while
  136.3 6.9 %copy-start.10 = (f32[128]{0:T(128)S(1)}, f32[128]{0:T(128)}, u32[]{:S(2)}) copy-start(f32[128]{0:T(128)} %get-tuple-element.1410) | copy-start | bytes 1540 | tf_op jit(solution)/shard_map/while
  136.3 6.9 %copy-start.13 = (f32[128]{0:T(128)S(1)}, f32[128]{0:T(128)}, u32[]{:S(2)}) copy-start(f32[128]{0:T(128)} %get-tuple-element.1409) | copy-start | bytes 1540 | tf_op jit(solution)/shard_map/while
  156.6 6.0 %copy-start.7 = (f32[64,128]{1,0:T(8,128)S(1)}, f32[64,128]{1,0:T(8,128)}, u32[]{:S(2)}) copy-start(f32[64,128]{1,0:T(8,128)} %get-tuple-element.1407) | copy-start | bytes 98308 | tf_op jit(solution)/shard_map/while
  156.6 6.0 %copy-start.20 = (f32[128]{0:T(128)S(1)}, f32[128]{0:T(128)}, u32[]{:S(2)}) copy-start(f32[128]{0:T(128)} %get-tuple-element.1447) | copy-start | bytes 1540 | tf_op jit(solution)/shard_map/while
  165.8 6.9 %copy-start.8 = (f32[64,128]{1,0:T(8,128)}, f32[64,128]{1,0:T(8,128)S(1)}, u32[]{:S(2)}) copy-start(f32[64,128]{1,0:T(8,128)S(1)} %fusion.96) | copy-start | bytes 98308 | tf_op jit(solution)/shard_map/while
  165.8 6.9 %copy-start.10 = (f32[128]{0:T(128)S(1)}, f32[128]{0:T(128)}, u32[]{:S(2)}) copy-start(f32[128]{0:T(128)} %get-tuple-element.1410) | copy-start | bytes 1540 | tf_op jit(solution)/shard_map/while
  165.8 6.9 %copy-start.13 = (f32[128]{0:T(128)S(1)}, f32[128]{0:T(128)}, u32[]{:S(2)}) copy-start(f32[128]{0:T(128)} %get-tuple-element.1409) | copy-start | bytes 1540 | tf_op jit(solution)/shard_map/while
  186.1 6.0 %copy-start.7 = (f32[64,128]{1,0:T(8,128)S(1)}, f32[64,128]{1,0:T(8,128)}, u32[]{:S(2)}) copy-start(f32[64,128]{1,0:T(8,128)} %get-tuple-element.1407) | copy-start | bytes 98308 | tf_op jit(solution)/shard_map/while
  186.1 6.0 %copy-start.20 = (f32[128]{0:T(128)S(1)}, f32[128]{0:T(128)}, u32[]{:S(2)}) copy-start(f32[128]{0:T(128)} %get-tuple-element.1447) | copy-start | bytes 1540 | tf_op jit(solution)/shard_map/while
  195.4 6.9 %copy-start.8 = (f32[64,128]{1,0:T(8,128)}, f32[64,128]{1,0:T(8,128)S(1)}, u32[]{:S(2)}) copy-start(f32[64,128]{1,0:T(8,128)S(1)} %fusion.96) | copy-start | bytes 98308 | tf_op jit(solution)/shard_map/while
  195.4 6.9 %copy-start.10 = (f32[128]{0:T(128)S(1)}, f32[128]{0:T(128)}, u32[]{:S(2)}) copy-start(f32[128]{0:T(128)} %get-tuple-element.1410) | copy-start | bytes 1540 | tf_op jit(solution)/shard_map/while
  195.4 6.9 %copy-start.13 = (f32[128]{0:T(128)S(1)}, f32[128]{0:T(128)}, u32[]{:S(2)}) copy-start(f32[128]{0:T(128)} %get-tuple-element.1409) | copy-start | bytes 1540 | tf_op jit(solution)/shard_map/while
  215.7 6.0 %copy-start.7 = (f32[64,128]{1,0:T(8,128)S(1)}, f32[64,128]{1,0:T(8,128)}, u32[]{:S(2)}) copy-start(f32[64,128]{1,0:T(8,128)} %get-tuple-element.1407) | copy-start | bytes 98308 | tf_op jit(solution)/shard_map/while
  215.7 6.0 %copy-start.20 = (f32[128]{0:T(128)S(1)}, f32[128]{0:T(128)}, u32[]{:S(2)}) copy-start(f32[128]{0:T(128)} %get-tuple-element.1447) | copy-start | bytes 1540 | tf_op jit(solution)/shard_map/while
  224.9 6.9 %copy-start.8 = (f32[64,128]{1,0:T(8,128)}, f32[64,128]{1,0:T(8,128)S(1)}, u32[]{:S(2)}) copy-start(f32[64,128]{1,0:T(8,128)S(1)} %fusion.96) | copy-start | bytes 98308 | tf_op jit(solution)/shard_map/while
  224.9 6.9 %copy-start.10 = (f32[128]{0:T(128)S(1)}, f32[128]{0:T(128)}, u32[]{:S(2)}) copy-start(f32[128]{0:T(128)} %get-tuple-element.1410) | copy-start | bytes 1540 | tf_op jit(solution)/shard_map/while
  224.9 6.9 %copy-start.13 = (f32[128]{0:T(128)S(1)}, f32[128]{0:T(128)}, u32[]{:S(2)}) copy-start(f32[128]{0:T(128)} %get-tuple-element.1409) | copy-start | bytes 1540 | tf_op jit(solution)/shard_map/while
  245.2 6.0 %copy-start.7 = (f32[64,128]{1,0:T(8,128)S(1)}, f32[64,128]{1,0:T(8,128)}, u32[]{:S(2)}) copy-start(f32[64,128]{1,0:T(8,128)} %get-tuple-element.1407) | copy-start | bytes 98308 | tf_op jit(solution)/shard_map/while
  254.5 6.9 %copy-start.8 = (f32[64,128]{1,0:T(8,128)}, f32[64,128]{1,0:T(8,128)S(1)}, u32[]{:S(2)}) copy-start(f32[64,128]{1,0:T(8,128)S(1)} %fusion.96) | copy-start | bytes 98308 | tf_op jit(solution)/shard_map/while
  254.5 6.9 %copy-start.10 = (f32[128]{0:T(128)S(1)}, f32[128]{0:T(128)}, u32[]{:S(2)}) copy-start(f32[128]{0:T(128)} %get-tuple-element.1410) | copy-start | bytes 1540 | tf_op jit(solution)/shard_map/while
  254.5 6.9 %copy-start.13 = (f32[128]{0:T(128)S(1)}, f32[128]{0:T(128)}, u32[]{:S(2)}) copy-start(f32[128]{0:T(128)} %get-tuple-element.1409) | copy-start | bytes 1540 | tf_op jit(solution)/shard_map/while
  274.8 6.0 %copy-start.7 = (f32[64,128]{1,0:T(8,128)S(1)}, f32[64,128]{1,0:T(8,128)}, u32[]{:S(2)}) copy-start(f32[64,128]{1,0:T(8,128)} %get-tuple-element.1407) | copy-start | bytes 98308 | tf_op jit(solution)/shard_map/while
  274.8 6.0 %copy-start.20 = (f32[128]{0:T(128)S(1)}, f32[128]{0:T(128)}, u32[]{:S(2)}) copy-start(f32[128]{0:T(128)} %get-tuple-element.1447) | copy-start | bytes 1540 | tf_op jit(solution)/shard_map/while
  284.0 6.9 %copy-start.8 = (f32[64,128]{1,0:T(8,128)}, f32[64,128]{1,0:T(8,128)S(1)}, u32[]{:S(2)}) copy-start(f32[64,128]{1,0:T(8,128)S(1)} %fusion.96) | copy-start | bytes 98308 | tf_op jit(solution)/shard_map/while
  284.0 6.9 %copy-start.10 = (f32[128]{0:T(128)S(1)}, f32[128]{0:T(128)}, u32[]{:S(2)}) copy-start(f32[128]{0:T(128)} %get-tuple-element.1410) | copy-start | bytes 1540 | tf_op jit(solution)/shard_map/while
  284.0 6.9 %copy-start.13 = (f32[128]{0:T(128)S(1)}, f32[128]{0:T(128)}, u32[]{:S(2)}) copy-start(f32[128]{0:T(128)} %get-tuple-element.1409) | copy-start | bytes 1540 | tf_op jit(solution)/shard_map/while
  304.3 6.0 %copy-start.7 = (f32[64,128]{1,0:T(8,128)S(1)}, f32[64,128]{1,0:T(8,128)}, u32[]{:S(2)}) copy-start(f32[64,128]{1,0:T(8,128)} %get-tuple-element.1407) | copy-start | bytes 98308 | tf_op jit(solution)/shard_map/while
  313.6 6.9 %copy-start.8 = (f32[64,128]{1,0:T(8,128)}, f32[64,128]{1,0:T(8,128)S(1)}, u32[]{:S(2)}) copy-start(f32[64,128]{1,0:T(8,128)S(1)} %fusion.96) | copy-start | bytes 98308 | tf_op jit(solution)/shard_map/while
  313.6 6.9 %copy-start.10 = (f32[128]{0:T(128)S(1)}, f32[128]{0:T(128)}, u32[]{:S(2)}) copy-start(f32[128]{0:T(128)} %get-tuple-element.1410) | copy-start | bytes 1540 | tf_op jit(solution)/shard_map/while
  313.6 6.9 %copy-start.13 = (f32[128]{0:T(128)S(1)}, f32[128]{0:T(128)}, u32[]{:S(2)}) copy-start(f32[128]{0:T(128)} %get-tuple-element.1409) | copy-start | bytes 1540 | tf_op jit(solution)/shard_map/while
  333.9 6.0 %copy-start.7 = (f32[64,128]{1,0:T(8,128)S(1)}, f32[64,128]{1,0:T(8,128)}, u32[]{:S(2)}) copy-start(f32[64,128]{1,0:T(8,128)} %get-tuple-element.1407) | copy-start | bytes 98308 | tf_op jit(solution)/shard_map/while
  343.1 6.9 %copy-start.8 = (f32[64,128]{1,0:T(8,128)}, f32[64,128]{1,0:T(8,128)S(1)}, u32[]{:S(2)}) copy-start(f32[64,128]{1,0:T(8,128)S(1)} %fusion.96) | copy-start | bytes 98308 | tf_op jit(solution)/shard_map/while
  343.1 6.9 %copy-start.10 = (f32[128]{0:T(128)S(1)}, f32[128]{0:T(128)}, u32[]{:S(2)}) copy-start(f32[128]{0:T(128)} %get-tuple-element.1410) | copy-start | bytes 1540 | tf_op jit(solution)/shard_map/while
  343.1 6.9 %copy-start.13 = (f32[128]{0:T(128)S(1)}, f32[128]{0:T(128)}, u32[]{:S(2)}) copy-start(f32[128]{0:T(128)} %get-tuple-element.1409) | copy-start | bytes 1540 | tf_op jit(solution)/shard_map/while
  353.8 167.5 %reduce-scatter.4.cloned.1.call-start = ((), (), s32[]{:S(2)}) async-start(), calls=%async_computation.3 | async-start | bytes 327680 | tf_op jit(solution)/shard_map/reduce_scatter | solution.py:163
  354.5 124.7 %copy-start.3 = (bf16[128,128]{1,0:T(8,128)(2,1)S(1)}, bf16[128,128]{1,0:T(8,128)(2,1)}, u32[]{:S(2)}) copy-start(bf16[128,128]{1,0:T(8,128)(2,1)} %param.26) | copy-start | bytes 98308
  479.2 42.1 %copy-start.4 = (bf16[2,64,128]{2,1,0:T(8,128)(2,1)S(1)}, bf16[2,64,128]{2,1,0:T(8,128)(2,1)}, u32[]{:S(2)}) copy-start(bf16[2,64,128]{2,1,0:T(8,128)(2,1)} %param.21) | copy-start | bytes 98308
  479.2 104.0 %copy-start.5 = (bf16[2,64,128]{2,1,0:T(8,128)(2,1)S(1)}, bf16[2,64,128]{2,1,0:T(8,128)(2,1)}, u32[]{:S(2)}) copy-start(bf16[2,64,128]{2,1,0:T(8,128)(2,1)} %param.31) | copy-start | bytes 98308
  479.2 43.5 %reduce-scatter.6.cloned.1.call-start = ((), (), s32[]{:S(2)}) async-start(), calls=%async_computation.4 | async-start | bytes 163840 | tf_op jit(solution)/shard_map/reduce_scatter | solution.py:211
  480.4 102.8 %reduce-scatter.8.cloned.1.call-start = ((), (), s32[]{:S(2)}) async-start(), calls=%async_computation.5 | async-start | bytes 294912 | tf_op jit(solution)/shard_map/reduce_scatter | solution.py:214
  (58 other events, 206.2 us)
Sparse Core Ops, SparseCore 0:
  353.9 114.9 all-reduce.2
Sparse Core Ops, SparseCore 1:
  479.3 17.3 reduce-scatter.3
  499.1 19.5 reduce-scatter.5
  521.8 61.3 reduce-scatter.7
where the time goes:
time: 598 us; the launch traced here: 592 us
  matrix products  177 us (30%)
  blocking collectives  138 us (23%)
  other arithmetic  75.2 us (13%)
  loops' own time  70.4 us (12%)
  waiting for transfers between devices  60.5 us (10%)
  local copies, waits for them, and re-layouts  55 us (9%)
  between operations  15.9 us (3%)
    dot_general x16, matrix products, tile_forward(): jnp.einsum('mh,hij->mij', w_second, hidden, preferred_element_type=jnp.fl...  90.5 us
    another operation x2, loops' own time, sweep(): return lax.fori_loop(0, groups, group_step, init)  70.4 us
    reduce_scatter x1, waiting for transfers between devices, per_device(): lax.psum_scatter(col_feat_grad.astype(jnp.bfloat16), 'row', scatter_dimen...  60.5 us
    dot_general x8, matrix products, tile_terms(): jnp.einsum('mh,mij->hij', w_second, grad_low, preferred_element_type=jnp....  54.8 us
    another operation x32, other arithmetic  38.9 us
    psum x1, blocking collectives, per_device(): lax.psum((local_first, grad_b1, grad_ds, grad_w2, grad_b2), ('row', 'col'))  37.7 us
    all_gather x1, blocking collectives, per_device(): lax.all_gather(feats, 'row', axis=0, tiled=True)  30.9 us
    all_gather x1, blocking collectives, per_device(): lax.all_gather(coords, 'row', axis=0, tiled=True)  26 us
  transfers between devices with their start and end apart: 4, of which 1 were waited for; matrix products, arithmetic and copies ran while one was open for 16% of the time, Pallas kernels for 0%

commit v1 on v0

v1 whole, which is shorter than its diff:
```python
import functools
import jax
import jax.numpy as jnp
from jax import lax
from jax.experimental import pallas as pl
from jax.experimental.pallas import tpu as pltpu
from jax.sharding import PartitionSpec as P

L = 64
H = 128
CP = 128
GROUP = 16
WIDE = GROUP * CP
CELLS = 2
NT = (((1,), (1,)), ((), ()))
NN = (((1,), (0,)), ((), ()))
F32 = jnp.float32
BF16 = jnp.bfloat16


def dot(a, b, dims=NN):
    return lax.dot_general(a, b, dims, preferred_element_type=F32)


def split(value):
    high = value.astype(BF16)
    return high, (value - high.astype(F32)).astype(BF16)


def dot_split(a, b, dims=NN):
    high, low = split(b)
    return dot(a, high, dims) + dot(a, low, dims)


def column(row, rows):
    return jnp.transpose(jnp.broadcast_to(row, (rows, row.shape[1])))


def pair_kernel(
    count_ref, pairs_ref,
    r_ref, c_ref,
    w1_ref, b1_ref, ds_ref, w2_ref, b2_ref,
    rows_ref, cola_ref, colb_ref, par_ref,
    lhs, rhs, sums_lhs, sq_s, env_s, base_s, y_s, slope_s, x3_s,
    racc, cacc, gcol, gw2, gds,
):
    n_row = r_ref.shape[0]
    n_col = c_ref.shape[0]
    me_row, me_col = lax.axis_index("row"), lax.axis_index("col")
    halves = n_col // (2 * CELLS)
    ring = n_row // CELLS

    def place(cell):
        source, inner = cell // CELLS, cell % CELLS
        step = lax.rem(source // 2 - me_row // 2 + halves, halves)
        return (step * 2 + lax.rem(source + me_row, 2)) * CELLS + inner

    lane = lax.broadcasted_iota(jnp.int32, (H, CP), 1)
    onehot = (
        lax.broadcasted_iota(jnp.int32, (GROUP, WIDE), 1) // CP
        == lax.broadcasted_iota(jnp.int32, (GROUP, WIDE), 0)
    ).astype(F32)
    hot = onehot.astype(BF16)
    rhs[0:GROUP, :] = hot
    rhs[GROUP:2 * GROUP, :] = hot
    rhs[2 * GROUP:3 * GROUP, :] = jnp.zeros((GROUP, WIDE), BF16)
    rhs[3 * GROUP:4 * GROUP, :] = hot
    sums_lhs[0:GROUP, :] = hot
    sums_lhs[GROUP:2 * GROUP, :] = jnp.zeros((GROUP, WIDE), BF16)
    racc[...] = jnp.zeros_like(racc)
    cacc[...] = jnp.zeros_like(cacc)
    gw2[...] = jnp.zeros_like(gw2)
    gds[...] = jnp.zeros_like(gds)
    b1_b = column(b1_ref[...], CP)
    ds_b = 0.5 * column(ds_ref[...], CP)
    b2_b = 0.5 * jnp.transpose(jnp.broadcast_to(b2_ref[...], (CP, 2 * L))[:, :])[:L, :]
    ds_hi = ds_b.astype(BF16).astype(F32)
    ds_lo = ds_b - ds_hi
    ds_part = jnp.where(lane < 34, ds_hi, jnp.where(lane < 35, ds_lo, 0.0))
    w1 = w1_ref[...]
    w1r = w1[:, :L]
    w1c = w1[:, L:]
    w2 = w2_ref[...]
    w2h = (0.5 * w2.astype(F32)).astype(BF16)
    w2t = jnp.transpose(0.5 * w2.astype(F32)).astype(BF16)

    def tile(index, carry):
        u = pairs_ref[index, 0]
        v = place(pairs_ref[index, 1])
        a = 0.5 * (dot(w1r, r_ref[u, 0:L, :]) + b1_b)
        base_s[...] = 0.5 * dot(w1c, c_ref[v, 0:L, :])
        a_hi = a.astype(BF16).astype(F32)
        a_lo = a - a_hi
        cot = 0.5 * r_ref[u, L:2 * L, :].astype(F32)
        for g in range(CP // GROUP):
            hi_g = pltpu.roll(a_hi, (CP - GROUP * g) % CP, 1)
            lo_g = pltpu.roll(a_lo, (CP + GROUP - GROUP * g) % CP, 1)
            lhs[g, 0:H, :] = jnp.where(lane < 16, hi_g, jnp.where(lane < 32, lo_g, ds_part))[:, :64].astype(BF16)
            co_g = pltpu.roll(cot, (CP + 48 - GROUP * g) % CP, 1)
            lhs[g, H:H + L, :] = jnp.where((lane[:L] >= 48) & (lane[:L] < 64), co_g, 0.0)[:, :64].astype(BF16)
        xu = r_ref[u, 2 * L:2 * L + 16, :].astype(F32)
        xv = c_ref[v, L:L + 16, :].astype(F32)
        sq = jnp.zeros((CP, CP), F32)
        for k in range(3):
            off = column(xu[k:k + 1, :], CP) - xv[k:k + 1, :]
            sq = sq + off * off
        sq_s[...] = sq
        mu = column(xu[3:4, :], CP)
        mv = xv[3:4, :]
        env_s[...] = mu * mv / ((1.0 + sq) * CP)
        gcol[...] = jnp.zeros_like(gcol)

        def group(g, carry):
            first = pl.multiple_of(g * GROUP, GROUP)
            flat = jnp.concatenate(
                [sq_s[pl.ds(first + i, 1), :] for i in range(GROUP)], axis=1
            )
            flat_hi = flat.astype(BF16).astype(F32)
            flat_lo = flat - flat_hi
            sub = lax.broadcasted_iota(jnp.int32, (GROUP, WIDE), 0)
            block = jnp.where(
                (sub == 0) | (sub == 2), flat_hi, jnp.where(sub == 1, flat_lo, 0.0)
            ).astype(BF16)
            rhs[2 * GROUP:3 * GROUP, :] = block
            block2 = jnp.where(sub == 0, flat_hi, jnp.where(sub == 1, flat_lo, 0.0)).astype(BF16)
            sums_lhs[GROUP:2 * GROUP, :] = block2
            z = dot(lhs[g], rhs[...])
            base = base_s[...]
            for i in range(GROUP):
                at = slice(i * CP, (i + 1) * CP)
                w = z[:H, at] + base
                t = jnp.tanh(w)
                p = 1.0 + t
                y_s[:, at] = (w * p).astype(BF16)
                slope_s[:, at] = (p * (1.0 + w * (1.0 - t))).astype(slope_s.dtype)
            pm = dot(w2h, y_s[...])
            for i in range(GROUP):
                at = slice(i * CP, (i + 1) * CP)
                w = pm[:, at] + b2_b
                t = jnp.tanh(w)
                p = 1.0 + t
                e = env_s[pl.ds(first + i, 1), :]
                x3_s[L:2 * L, at] = (w * p * e).astype(BF16)
                x3_s[0:L, at] = (p * (1.0 + w * (1.0 - t)) * (z[H:, at] * e)).astype(BF16)
            gh = dot(w2t, x3_s[0:L, :])
            total = gcol[...]
            for i in range(GROUP):
                at = slice(i * CP, (i + 1) * CP)
                inner = gh[:, at] * slope_s[:, at]
                total = total + inner
                x3_s[2 * L:, at] = inner.astype(BF16)
            gcol[...] = total
            gw2[...] += dot(x3_s[0:L, :], y_s[...], NT)
            s = dot(sums_lhs[...], x3_s[...], NT)
            racc[u, pl.ds(first, GROUP), :] += s[:GROUP]
            gds[...] += s[GROUP:GROUP + 8]
            return carry

        lax.fori_loop(0, CP // GROUP, group, 0)
        cacc[v] += gcol[...]
        return carry

    lax.fori_loop(0, count_ref[0], tile, 0)

    w1rt = jnp.transpose(w1r.astype(F32)).astype(BF16)
    w1ct = jnp.transpose(w1c.astype(F32)).astype(BF16)

    def finish_row(c, carry):
        first, bias1, bias2 = carry
        acc = racc[c]
        out = lax.rem(c // CELLS - me_col + ring, ring) * CELLS + c % CELLS
        rows_ref[out, 0:L, :] = jnp.transpose(acc[:, L:2 * L]).astype(rows_ref.dtype)
        grads = acc[:, 2 * L:]
        rows_ref[out, L:2 * L, :] = dot_split(w1rt, grads, NT).astype(rows_ref.dtype)
        first = first + dot_split(r_ref[c, 0:L, :], grads)
        bias1 = bias1 + jnp.sum(grads, axis=0, keepdims=True)
        bias2 = bias2 + jnp.sum(acc[:, :2 * L], axis=0, keepdims=True)
        return first, bias1, bias2

    first_r, bias1, bias2 = lax.fori_loop(
        0, n_row, finish_row,
        (jnp.zeros((L, H), F32), jnp.zeros((1, H), F32), jnp.zeros((1, 2 * L), F32)),
    )

    def finish_col(c, first):
        grads = cacc[c]
        value = dot_split(w1ct, grads)
        slot, inner = c // CELLS, c % CELLS

        @pl.when(slot % 2 == 0)
        def _():
            colb_ref[(slot // 2) * CELLS + inner] = value

        @pl.when(slot % 2 == 1)
        def _():
            cola_ref[(slot // 2) * CELLS + inner] = value.astype(cola_ref.dtype)

        return first + dot_split(c_ref[c, 0:L, :], grads, NT)

    first_c = lax.fori_loop(0, n_col, finish_col, jnp.zeros((L, H), F32))
    par_ref[0:L, :] = first_r
    par_ref[L:2 * L, :] = first_c
    par_ref[2 * L:3 * L, :] = gw2[...]
    par_ref[3 * L:3 * L + 8, :] = jnp.zeros((8, H), F32)
    par_ref[3 * L:3 * L + 1, :] = bias1
    par_ref[3 * L + 1:3 * L + 2, :] = gds[0:1, 2 * L:] + gds[1:2, 2 * L:]
    par_ref[3 * L + 2:3 * L + 3, :] = bias2


def pair_call(count, pairs, rp, cp, w1, b1, ds, w2, b2):
    n_row, n_col = rp.shape[0], cp.shape[0]
    vm = pl.BlockSpec(memory_space=pltpu.VMEM)
    sm = pl.BlockSpec(memory_space=pltpu.SMEM)
    b2p = jnp.pad(b2, (0, 2 * L - b2.shape[0]))
    return pl.pallas_call(
        pair_kernel,
        out_shape=(
            jax.ShapeDtypeStruct((n_row, 2 * L, CP), BF16),
            jax.ShapeDtypeStruct((n_col // 2, L, CP), BF16),
            jax.ShapeDtypeStruct((n_col // 2, L, CP), F32),
            jax.ShapeDtypeStruct((3 * L + 8, H), F32),
        ),
        in_specs=[sm, sm] + [vm] * 7,
        out_specs=(vm, vm, vm, vm),
        scratch_shapes=[
            pltpu.VMEM((CP // GROUP, H + L, 64), BF16),
            pltpu.VMEM((4 * GROUP, WIDE), BF16),
            pltpu.VMEM((2 * GROUP, WIDE), BF16),
            pltpu.VMEM((CP, CP), F32),
            pltpu.VMEM((CP, CP), F32),
            pltpu.VMEM((H, CP), F32),
            pltpu.VMEM((H, WIDE), BF16),
            pltpu.VMEM((H, WIDE), F32),
            pltpu.VMEM((2 * H, WIDE), BF16),
            pltpu.VMEM((n_row, CP, 2 * H), F32),
            pltpu.VMEM((n_col, H, CP), F32),
            pltpu.VMEM((H, CP), F32),
            pltpu.VMEM((L, H), F32),
            pltpu.VMEM((8, 2 * H), F32),
        ],
        compiler_params=pltpu.CompilerParams(vmem_limit_bytes=32 * 1024 * 1024),
        name="pair_tiles",
    )(count, pairs, rp, cp, w1, b1.reshape(1, H), ds.reshape(1, H), w2, b2p.reshape(1, 2 * L))


def stepped(n, d):
    return [(i, (i + 2 * d) % n) for i in range(n)]


def per_device(
    feats, coords, valid, pairs, pair_count, w_first, bias_first, dist_scale,
    w_second, bias_second, cotangent, rows_n, cols_n,
):
    swap = [(i, i ^ 1) for i in range(rows_n)]
    halves = rows_n // 2
    extra = jnp.concatenate(
        [coords, valid.astype(BF16)[:, None], jnp.zeros((CELLS, 12, CP), BF16)], axis=1
    )
    col_own = jnp.concatenate([feats, extra], axis=1)
    row_own = jnp.concatenate([feats, cotangent, extra], axis=1)
    col_pair = jnp.concatenate([col_own, lax.ppermute(col_own, "row", swap)], axis=0)
    col_parts = [col_pair] + [
        lax.ppermute(col_pair, "row", stepped(rows_n, -d)) for d in range(1, halves)
    ]
    row_pack = lax.all_gather(row_own, "col", axis=0, tiled=True)
    col_pack = jnp.concatenate(col_parts, axis=0)
    rows_out, cola, colb, par = pair_call(
        pair_count[0], pairs[0, 0], row_pack, col_pack,
        w_first, bias_first, dist_scale, w_second, bias_second,
    )
    got_rows = [rows_out[:CELLS].astype(F32)]
    for d in range(1, cols_n):
        move = [(i, (i + d) % cols_n) for i in range(cols_n)]
        got_rows.append(
            lax.ppermute(rows_out[d * CELLS:(d + 1) * CELLS], "col", move).astype(F32)
        )
    own_rows = sum(got_rows)
    cola = lax.ppermute(cola, "row", swap)
    par = par + lax.ppermute(par, "row", swap)
    col_half = colb + cola.astype(F32)
    col_send = col_half.astype(BF16)
    own_cols = col_half[:CELLS]
    total = par
    for d in range(1, halves):
        own_cols = own_cols + lax.ppermute(
            col_send[d * CELLS:(d + 1) * CELLS], "row", stepped(rows_n, d)
        ).astype(F32)
        total = total + lax.ppermute(par, "row", stepped(rows_n, d))
    par = total
    for d in range(1, cols_n):
        move = [(i, (i + d) % cols_n) for i in range(cols_n)]
        total = total + lax.ppermute(par, "col", move)
    updated = (feats.astype(F32) + own_rows[:, :L]).astype(BF16)
    grad_feats = cotangent.astype(F32) + own_rows[:, L:] + own_cols
    return (
        updated,
        grad_feats,
        jnp.transpose(total[:2 * L]),
        total[3 * L],
        total[3 * L + 1],
        total[2 * L:3 * L],
        total[3 * L + 2, :L],
    )


def solution(mesh):
    spread = P(("row", "col"))
    placed = (spread, spread, spread, P("row", "col"), P("row", "col"), P(), P(), P(), P(), P(), spread)
    return jax.shard_map(
        functools.partial(per_device, rows_n=mesh.shape["row"], cols_n=mesh.shape["col"]),
        mesh=mesh,
        in_specs=placed,
        out_specs=(spread, spread, P(), P(), P(), P(), P()),
        check_vma=False,
    )
```

time: 598 us -> 160 us (0.27)
  matrix products: 177 us -> 0 us
  blocking collectives: 138 us -> 5.92 us
  starting transfers between devices: 0.17 us -> 108 us
  other arithmetic: 75.2 us -> 2.36 us
  loops' own time: 70.4 us -> 0 us
  local copies, waits for them, and re-layouts: 55 us -> 4.15 us
  waiting for transfers between devices: 60.5 us -> 15.7 us
  Pallas kernels: 0 us -> 20.3 us
  between operations: 15.9 us -> 1.52 us
    dot_general x38 -> x0, matrix products: 177 us -> none  [the longest x16 90.5 us: tile_forward(): jnp.einsum('mh,hij->mij', w_second, hidden, preferred_element_type=jnp.fl...]
    ppermute x0 -> x18, starting transfers between devices: none -> 108 us  [the longest x3 50.7 us: per_device(): lax.ppermute(rows_out[d * CELLS:(d + 1) * CELLS], 'col', move).astype(F32)]
    all_gather x7 -> x1, blocking collectives: 101 us -> 5.92 us  [per_device(): row_pack = lax.all_gather(row_own, 'col', axis=0, tiled=True)]
    another operation x2 -> x0, loops' own time: 70.4 us -> none  [sweep(): return lax.fori_loop(0, groups, group_step, init)]
    reduce_scatter x3 -> x0, waiting for transfers between devices: 60.5 us -> none  [the longest x1 60.5 us: per_device(): lax.psum_scatter(col_feat_grad.astype(jnp.bfloat16), 'row', scatter_dimen...]
    another operation x32 -> x0, other arithmetic: 38.9 us -> none
    psum x1 -> x0, blocking collectives: 37.7 us -> none  [per_device(): lax.psum((local_first, grad_b1, grad_ds, grad_w2, grad_b2), ('row', 'col'))]
    pallas_call x0 -> x1, Pallas kernels: none -> 20.3 us  [pair_call(): pl.pallas_call(pair_kernel, out_shape=(jax.ShapeDtypeStruct((n_row, 2 * L...]
  transfers between devices with their start and end apart: 4 -> 18, of which waited for: 1 -> 4; matrix products, arithmetic and copies ran while one was open for 16% -> 1% of each run, Pallas kernels for 0% -> 0%
where the time goes in v1:
time: 160 us; the launch traced here: 158 us
  starting transfers between devices  108 us (68%)
  Pallas kernels  20.3 us (13%)
  waiting for transfers between devices  15.7 us (10%)
  blocking collectives  5.92 us (4%)
  local copies, waits for them, and re-layouts  4.15 us (3%)
  other arithmetic  2.36 us (1%)
    ppermute x3, starting transfers between devices, per_device(): lax.ppermute(rows_out[d * CELLS:(d + 1) * CELLS], 'col', move).astype(F32)  50.7 us
    ppermute x1, starting transfers between devices, per_device(): par = par + lax.ppermute(par, 'row', swap)  25.7 us
    pallas_call x1, Pallas kernels, pair_call(): pl.pallas_call(pair_kernel, out_shape=(jax.ShapeDtypeStruct((n_row, 2 * L...  20.3 us
    ppermute x3, starting transfers between devices, per_device(): total = total + lax.ppermute(par, 'row', stepped(rows_n, d))  16.7 us
    all_gather x1, blocking collectives, per_device(): row_pack = lax.all_gather(row_own, 'col', axis=0, tiled=True)  5.92 us
    ppermute x3, starting transfers between devices, per_device(): lax.ppermute(col_pair, 'row', stepped(rows_n, -d))  5.57 us
    ppermute x3, waiting for transfers between devices, per_device(): total = total + lax.ppermute(par, 'col', move)  4.82 us
    ppermute x3, waiting for transfers between devices, per_device(): lax.ppermute(col_pair, 'row', stepped(rows_n, -d))  4.74 us
  transfers between devices with their start and end apart: 18, of which 4 were waited for; matrix products, arithmetic and copies ran while one was open for 1% of the time, Pallas kernels for 0%

profile of v1, /device:TPU:0, one launch (start us, length us, event | category | flops | bytes accessed | tf_op | source)
XLA Modules:
  0.0 158.3 jit_solution(11047564957096527160)
XLA Ops:
  0.6 0.7 convert_bitcast_fusion
  1.4 0.0 copy-start.4
  1.4 0.0 copy-start.5
  1.4 0.8 pad_maximum_fusion.1
  2.2 0.0 copy-start.8
  2.2 3.0 %collective-permute-start = (bf16[2,80,128]{2,1,0:T(8,128)(2,1)S(1)}, bf16[2,80,128]{2,1,0:T(8,128)(2,1)S(1)}, u32[]{:S(2)}, u32[]{:S(2)}) collective-permute-start(bf16[2,80,128]{2,1,0:T(8,128)(2,1)S(1)} %get-tuple-element.48), channel_id=1, source_target_pairs={{0,4},{4,0},{8,12},{12,8},{16,20},{20,16},{24,28},{28,24},{1,5},{5... | collective-permute-start | bytes 122888 | tf_op jit(solution)/shard_map/ppermute | solution.py:261
  5.3 0.2 concatenate.16
  5.5 5.9 %all_gather.3.r_ref = bf16[8,144,128]{2,1,0:T(8,128)(2,1)S(1)} all-gather(bf16[2,144,128]{2,1,0:T(8,128)(2,1)S(1)} %concatenate.16), channel_id=1, replica_groups=mesh['row'=8,'col'=4] {'col'}, dimensions={0}, use_global_device_ids=true | all-gather | bytes 368640 | tf_op jit(solution)/shard_map/all_gather | solution.py:265
  12.0 0.0 copy-start.7
  12.0 0.7 copy-done.7
  12.7 0.1 copy.32.pairs_ref
  12.8 1.6 %collective-permute-start.3 = (bf16[4,80,128]{2,1,0:T(8,128)(2,1)S(1)}, bf16[4,80,128]{2,1,0:T(8,128)(2,1)S(1)}, u32[]{:S(2)}, u32[]{:S(2)}) collective-permute-start(bf16[4,80,128]{2,1,0:T(8,128)(2,1)S(1)} %pad_maximum_fusion), channel_id=1, source_target_pairs={{0,8},{4,12},{8,16},{12,20},{16,24},{20,28},{24,0},{28,4},{1,9},{5... | collective-permute-start | bytes 245768 | tf_op jit(solution)/shard_map/ppermute | solution.py:263
  14.4 2.6 %collective-permute-start.2 = (bf16[4,80,128]{2,1,0:T(8,128)(2,1)S(1)}, bf16[4,80,128]{2,1,0:T(8,128)(2,1)S(1)}, u32[]{:S(2)}, u32[]{:S(2)}) collective-permute-start(bf16[4,80,128]{2,1,0:T(8,128)(2,1)S(1)} %pad_maximum_fusion), channel_id=1, source_target_pairs={{0,16},{4,20},{8,24},{12,28},{16,0},{20,4},{24,8},{28,12},{1,17},{... | collective-permute-start | bytes 245768 | tf_op jit(solution)/shard_map/ppermute | solution.py:263
  17.0 1.3 collective-permute-start.1
  18.4 4.7 %collective-permute-done.1 = bf16[4,80,128]{2,1,0:T(8,128)(2,1)S(1)} collective-permute-done((bf16[4,80,128]{2,1,0:T(8,128)(2,1)S(1)}, bf16[4,80,128]{2,1,0:T(8,128)(2,1)S(1)}, u32[]{:S(2)}, u32[]{:S(2)}) %collective-permute-start.1) | collective-permute-done | bytes 81952 | tf_op jit(solution)/shard_map/ppermute | solution.py:263
  23.1 0.0 collective-permute-done.2
  23.2 0.0 copy-start
  23.2 0.0 collective-permute-done.3
  23.2 0.0 copy-start.1
  23.2 0.0 copy-start.2
  23.2 0.0 copy-start.3
  23.3 0.7 copy-done
  24.0 20.3 %pair_tiles.1 = (bf16[8,128,128]{2,1,0:T(8,128)(2,1)S(1)}, bf16[8,64,128]{2,1,0:T(8,128)(2,1)S(1)}, f32[8,64,128]{2,1,0:T(8,128)S(1)}, f32[200,128]{1,0:T(8,128)S(1)}) custom-call(s32[1]{0:T(128)} %bitcast.16.count_ref, s32[8,2]{1,0:T(8,128)S(1)} %copy.32.pairs_ref, bf16[8,144,128]{2,1,0:T(8,128)(2,1)S(1)} %all_gather.3.r_ref, ...), custom_call_target="tpu_custom_call" | custom-call | tf_op jit(solution)/shard_map/pair_tiles/pallas_call | solution.py:215
  44.3 0.1 collective-permute-start.4
  44.4 50.3 %collective-permute-start.6 = (bf16[2,128,128]{2,1,0:T(8,128)(2,1)S(1)}, bf16[2,128,128]{2,1,0:T(8,128)(2,1)S(1)}, u32[]{:S(2)}, u32[]{:S(2)}) collective-permute-start(bf16[2,128,128]{2,1,0:T(8,128)(2,1)S(1)} %get-tuple-element.39), channel_id=1, source_target_pairs={{0,3},{1,0},{2,1},{3,2},{4,7},{5,4},{6,5},{7,6},{8,11},{9,8},{10,9... | collective-permute-start | bytes 196616 | tf_op jit(solution)/shard_map/ppermute | solution.py:275
  94.7 0.3 collective-permute-start.5
  95.1 25.7 %collective-permute-start.11 = (f32[200,128]{1,0:T(8,128)S(1)}, f32[200,128]{1,0:T(8,128)S(1)}, u32[]{:S(2)}, u32[]{:S(2)}) collective-permute-start(f32[200,128]{1,0:T(8,128)S(1)} %get-tuple-element.14), channel_id=1, source_target_pairs={{0,4},{4,0},{8,12},{12,8},{16,20},{20,16},{24,28},{28,24},{1,5},{5... | collective-permute-start | bytes 307208 | tf_op jit(solution)/shard_map/ppermute | solution.py:279
  120.8 0.0 collective-permute-start.7
  120.8 0.0 collective-permute-done.4
  120.9 3.6 %collective-permute-done.11 = f32[200,128]{1,0:T(8,128)S(1)} collective-permute-done((f32[200,128]{1,0:T(8,128)S(1)}, f32[200,128]{1,0:T(8,128)S(1)}, u32[]{:S(2)}, u32[]{:S(2)}) %collective-permute-start.11) | collective-permute-done | bytes 102432 | tf_op jit(solution)/shard_map/ppermute | solution.py:279
  124.5 0.1 collective-permute-start.14
  124.5 14.7 %collective-permute-start.13 = (f32[200,128]{1,0:T(8,128)S(1)}, f32[200,128]{1,0:T(8,128)S(1)}, u32[]{:S(2)}, u32[]{:S(2)}) collective-permute-start(f32[200,128]{1,0:T(8,128)S(1)} %add.63), channel_id=1, source_target_pairs={{0,16},{4,20},{8,24},{12,28},{16,0},{20,4},{24,8},{28,12},{1,17},{... | collective-permute-start | bytes 307208 | tf_op jit(solution)/shard_map/ppermute | solution.py:288
  139.2 1.9 %collective-permute-start.12 = (f32[200,128]{1,0:T(8,128)S(1)}, f32[200,128]{1,0:T(8,128)S(1)}, u32[]{:S(2)}, u32[]{:S(2)}) collective-permute-start(f32[200,128]{1,0:T(8,128)S(1)} %add.63), channel_id=1, source_target_pairs={{0,8},{4,12},{8,16},{12,20},{16,24},{20,28},{24,0},{28,4},{1,9},{5... | collective-permute-start | bytes 307208 | tf_op jit(solution)/shard_map/ppermute | solution.py:288
  141.2 0.0 collective-permute-done.7
  141.3 0.1 collective-permute-start.8
  141.3 3.8 %collective-permute-start.10 = (bf16[2,64,128]{2,1,0:T(8,128)(2,1)S(1)}, bf16[2,64,128]{2,1,0:T(8,128)(2,1)S(1)}, u32[]{:S(2)}, u32[]{:S(2)}) collective-permute-start(bf16[2,64,128]{2,1,0:T(8,128)(2,1)S(1)} %get-tuple-element.44), channel_id=1, source_target_pairs={{0,24},{4,28},{8,0},{12,4},{16,8},{20,12},{24,16},{28,20},{1,25},{... | collective-permute-start | bytes 98312 | tf_op jit(solution)/shard_map/ppermute | solution.py:285
  145.1 2.5 %collective-permute-done.13 = f32[200,128]{1,0:T(8,128)S(1)} collective-permute-done((f32[200,128]{1,0:T(8,128)S(1)}, f32[200,128]{1,0:T(8,128)S(1)}, u32[]{:S(2)}, u32[]{:S(2)}) %collective-permute-start.13) | collective-permute-done | bytes 102432 | tf_op jit(solution)/shard_map/ppermute | solution.py:288
  147.7 0.0 collective-permute-done.12
  147.7 0.1 collective-permute-start.17
  147.8 2.4 %collective-permute-start.16 = (f32[200,128]{1,0:T(8,128)S(1)}, f32[200,128]{1,0:T(8,128)S(1)}, u32[]{:S(2)}, u32[]{:S(2)}) collective-permute-start(f32[200,128]{1,0:T(8,128)S(1)} %add_add_fusion.1), channel_id=1, source_target_pairs={{0,2},{1,3},{2,0},{3,1},{4,6},{5,7},{6,4},{7,5},{8,10},{9,11},{10,... | collective-permute-start | bytes 307208 | tf_op jit(solution)/shard_map/ppermute | solution.py:292
  150.2 0.0 collective-permute-done.8
  150.2 0.2 collective-permute-start.15
  150.4 0.7 fusion.2
  151.0 4.8 %collective-permute-done.16 = f32[200,128]{1,0:T(8,128)S(1)} collective-permute-done((f32[200,128]{1,0:T(8,128)S(1)}, f32[200,128]{1,0:T(8,128)S(1)}, u32[]{:S(2)}, u32[]{:S(2)}) %collective-permute-start.16) | collective-permute-done | bytes 102432 | tf_op jit(solution)/shard_map/ppermute | solution.py:292
  155.9 0.5 slice_bitcast_fusion.1
  156.4 0.5 slice_bitcast_fusion.2
  156.9 0.6 slice.69
  157.5 0.7 copy.33
  (34 shorter events, 0.3 us)
Async XLA Ops:
  0.6 0.7 copy-start.6
  1.4 3.9 %copy-start.4 = (bf16[2,64,128]{2,1,0:T(8,128)(2,1)S(1)}, bf16[2,64,128]{2,1,0:T(8,128)(2,1)}, u32[]{:S(2)}) copy-start(bf16[2,64,128]{2,1,0:T(8,128)(2,1)} %param.11) | copy-start | bytes 98308
  1.4 3.9 %copy-start.5 = (bf16[2,64,128]{2,1,0:T(8,128)(2,1)S(1)}, bf16[2,64,128]{2,1,0:T(8,128)(2,1)}, u32[]{:S(2)}) copy-start(bf16[2,64,128]{2,1,0:T(8,128)(2,1)} %param.21) | copy-start | bytes 98308
  2.2 3.0 %copy-start.8 = (f32[64]{0:T(128)S(1)}, f32[64]{0:T(128)}, u32[]{:S(2)}) copy-start(f32[64]{0:T(128)} %param.20) | copy-start | bytes 772
  2.2 10.6 %collective-permute-start = (bf16[2,80,128]{2,1,0:T(8,128)(2,1)S(1)}, bf16[2,80,128]{2,1,0:T(8,128)(2,1)S(1)}, u32[]{:S(2)}, u32[]{:S(2)}) collective-permute-start(bf16[2,80,128]{2,1,0:T(8,128)(2,1)S(1)} %get-tuple-element.48), channel_id=1, source_target_pairs={{0,4},{4,0},{8,12},{12,8},{16,20},{20,16},{24,28},{28,24},{1,5},{5... | collective-permute-start | bytes 122888 | tf_op jit(solution)/shard_map/ppermute | solution.py:261
  12.0 0.7 copy-start.7
  12.8 10.4 %collective-permute-start.3 = (bf16[4,80,128]{2,1,0:T(8,128)(2,1)S(1)}, bf16[4,80,128]{2,1,0:T(8,128)(2,1)S(1)}, u32[]{:S(2)}, u32[]{:S(2)}) collective-permute-start(bf16[4,80,128]{2,1,0:T(8,128)(2,1)S(1)} %pad_maximum_fusion), channel_id=1, source_target_pairs={{0,8},{4,12},{8,16},{12,20},{16,24},{20,28},{24,0},{28,4},{1,9},{5... | collective-permute-start | bytes 245768 | tf_op jit(solution)/shard_map/ppermute | solution.py:263
  14.4 8.7 %collective-permute-start.2 = (bf16[4,80,128]{2,1,0:T(8,128)(2,1)S(1)}, bf16[4,80,128]{2,1,0:T(8,128)(2,1)S(1)}, u32[]{:S(2)}, u32[]{:S(2)}) collective-permute-start(bf16[4,80,128]{2,1,0:T(8,128)(2,1)S(1)} %pad_maximum_fusion), channel_id=1, source_target_pairs={{0,16},{4,20},{8,24},{12,28},{16,0},{20,4},{24,8},{28,12},{1,17},{... | collective-permute-start | bytes 245768 | tf_op jit(solution)/shard_map/ppermute | solution.py:263
  17.0 6.1 %collective-permute-start.1 = (bf16[4,80,128]{2,1,0:T(8,128)(2,1)S(1)}, bf16[4,80,128]{2,1,0:T(8,128)(2,1)S(1)}, u32[]{:S(2)}, u32[]{:S(2)}) collective-permute-start(bf16[4,80,128]{2,1,0:T(8,128)(2,1)S(1)} %pad_maximum_fusion), channel_id=1, source_target_pairs={{0,24},{4,28},{8,0},{12,4},{16,8},{20,12},{24,16},{28,20},{1,25},{... | collective-permute-start | bytes 245768 | tf_op jit(solution)/shard_map/ppermute | solution.py:263
  23.2 0.8 copy-start
  23.2 0.7 copy-start.1
  23.2 0.7 copy-start.2
  23.2 0.7 copy-start.3
  44.3 76.5 %collective-permute-start.4 = (bf16[2,128,128]{2,1,0:T(8,128)(2,1)S(1)}, bf16[2,128,128]{2,1,0:T(8,128)(2,1)S(1)}, u32[]{:S(2)}, u32[]{:S(2)}) collective-permute-start(bf16[2,128,128]{2,1,0:T(8,128)(2,1)S(1)} %get-tuple-element.38), channel_id=1, source_target_pairs={{0,1},{1,2},{2,3},{3,0},{4,5},{5,6},{6,7},{7,4},{8,9},{9,10},{10,1... | collective-permute-start | bytes 196616 | tf_op jit(solution)/shard_map/ppermute | solution.py:275
  44.4 76.4 %collective-permute-start.6 = (bf16[2,128,128]{2,1,0:T(8,128)(2,1)S(1)}, bf16[2,128,128]{2,1,0:T(8,128)(2,1)S(1)}, u32[]{:S(2)}, u32[]{:S(2)}) collective-permute-start(bf16[2,128,128]{2,1,0:T(8,128)(2,1)S(1)} %get-tuple-element.39), channel_id=1, source_target_pairs={{0,3},{1,0},{2,1},{3,2},{4,7},{5,4},{6,5},{7,6},{8,11},{9,8},{10,9... | collective-permute-start | bytes 196616 | tf_op jit(solution)/shard_map/ppermute | solution.py:275
  94.7 26.1 %collective-permute-start.5 = (bf16[2,128,128]{2,1,0:T(8,128)(2,1)S(1)}, bf16[2,128,128]{2,1,0:T(8,128)(2,1)S(1)}, u32[]{:S(2)}, u32[]{:S(2)}) collective-permute-start(bf16[2,128,128]{2,1,0:T(8,128)(2,1)S(1)} %get-tuple-element.40), channel_id=1, source_target_pairs={{0,2},{1,3},{2,0},{3,1},{4,6},{5,7},{6,4},{7,5},{8,10},{9,11},{10,... | collective-permute-start | bytes 196616 | tf_op jit(solution)/shard_map/ppermute | solution.py:275
  95.1 29.4 %collective-permute-start.11 = (f32[200,128]{1,0:T(8,128)S(1)}, f32[200,128]{1,0:T(8,128)S(1)}, u32[]{:S(2)}, u32[]{:S(2)}) collective-permute-start(f32[200,128]{1,0:T(8,128)S(1)} %get-tuple-element.14), channel_id=1, source_target_pairs={{0,4},{4,0},{8,12},{12,8},{16,20},{20,16},{24,28},{28,24},{1,5},{5... | collective-permute-start | bytes 307208 | tf_op jit(solution)/shard_map/ppermute | solution.py:279
  120.8 20.4 %collective-permute-start.7 = (bf16[8,64,128]{2,1,0:T(8,128)(2,1)S(1)}, bf16[8,64,128]{2,1,0:T(8,128)(2,1)S(1)}, u32[]{:S(2)}, u32[]{:S(2)}) collective-permute-start(bf16[8,64,128]{2,1,0:T(8,128)(2,1)S(1)} %get-tuple-element.13), channel_id=1, source_target_pairs={{0,4},{4,0},{8,12},{12,8},{16,20},{20,16},{24,28},{28,24},{1,5},{5... | collective-permute-start | bytes 393224 | tf_op jit(solution)/shard_map/ppermute | solution.py:278
  124.5 20.7 %collective-permute-start.14 = (f32[200,128]{1,0:T(8,128)S(1)}, f32[200,128]{1,0:T(8,128)S(1)}, u32[]{:S(2)}, u32[]{:S(2)}) collective-permute-start(f32[200,128]{1,0:T(8,128)S(1)} %add.63), channel_id=1, source_target_pairs={{0,24},{4,28},{8,0},{12,4},{16,8},{20,12},{24,16},{28,20},{1,25},{... | collective-permute-start | bytes 307208 | tf_op jit(solution)/shard_map/ppermute | solution.py:288
  124.5 23.2 %collective-permute-start.13 = (f32[200,128]{1,0:T(8,128)S(1)}, f32[200,128]{1,0:T(8,128)S(1)}, u32[]{:S(2)}, u32[]{:S(2)}) collective-permute-start(f32[200,128]{1,0:T(8,128)S(1)} %add.63), channel_id=1, source_target_pairs={{0,16},{4,20},{8,24},{12,28},{16,0},{20,4},{24,8},{28,12},{1,17},{... | collective-permute-start | bytes 307208 | tf_op jit(solution)/shard_map/ppermute | solution.py:288
  139.2 8.4 %collective-permute-start.12 = (f32[200,128]{1,0:T(8,128)S(1)}, f32[200,128]{1,0:T(8,128)S(1)}, u32[]{:S(2)}, u32[]{:S(2)}) collective-permute-start(f32[200,128]{1,0:T(8,128)S(1)} %add.63), channel_id=1, source_target_pairs={{0,8},{4,12},{8,16},{12,20},{16,24},{20,28},{24,0},{28,4},{1,9},{5... | collective-permute-start | bytes 307208 | tf_op jit(solution)/shard_map/ppermute | solution.py:288
  141.3 8.9 %collective-permute-start.8 = (bf16[2,64,128]{2,1,0:T(8,128)(2,1)S(1)}, bf16[2,64,128]{2,1,0:T(8,128)(2,1)S(1)}, u32[]{:S(2)}, u32[]{:S(2)}) collective-permute-start(bf16[2,64,128]{2,1,0:T(8,128)(2,1)S(1)} %get-tuple-element.43), channel_id=1, source_target_pairs={{0,8},{4,12},{8,16},{12,20},{16,24},{20,28},{24,0},{28,4},{1,9},{5... | collective-permute-start | bytes 98312 | tf_op jit(solution)/shard_map/ppermute | solution.py:285
  141.3 9.0 %collective-permute-start.10 = (bf16[2,64,128]{2,1,0:T(8,128)(2,1)S(1)}, bf16[2,64,128]{2,1,0:T(8,128)(2,1)S(1)}, u32[]{:S(2)}, u32[]{:S(2)}) collective-permute-start(bf16[2,64,128]{2,1,0:T(8,128)(2,1)S(1)} %get-tuple-element.44), channel_id=1, source_target_pairs={{0,24},{4,28},{8,0},{12,4},{16,8},{20,12},{24,16},{28,20},{1,25},{... | collective-permute-start | bytes 98312 | tf_op jit(solution)/shard_map/ppermute | solution.py:285
  145.1 5.2 %collective-permute-start.9 = (bf16[2,64,128]{2,1,0:T(8,128)(2,1)S(1)}, bf16[2,64,128]{2,1,0:T(8,128)(2,1)S(1)}, u32[]{:S(2)}, u32[]{:S(2)}) collective-permute-start(bf16[2,64,128]{2,1,0:T(8,128)(2,1)S(1)} %get-tuple-element.45), channel_id=1, source_target_pairs={{0,16},{4,20},{8,24},{12,28},{16,0},{20,4},{24,8},{28,12},{1,17},{... | collective-permute-start | bytes 98312 | tf_op jit(solution)/shard_map/ppermute | solution.py:285
  147.7 3.3 %collective-permute-start.17 = (f32[200,128]{1,0:T(8,128)S(1)}, f32[200,128]{1,0:T(8,128)S(1)}, u32[]{:S(2)}, u32[]{:S(2)}) collective-permute-start(f32[200,128]{1,0:T(8,128)S(1)} %add_add_fusion.1), channel_id=1, source_target_pairs={{0,3},{1,0},{2,1},{3,2},{4,7},{5,4},{6,5},{7,6},{8,11},{9,8},{10,9... | collective-permute-start | bytes 307208 | tf_op jit(solution)/shard_map/ppermute | solution.py:292
  147.8 8.1 %collective-permute-start.16 = (f32[200,128]{1,0:T(8,128)S(1)}, f32[200,128]{1,0:T(8,128)S(1)}, u32[]{:S(2)}, u32[]{:S(2)}) collective-permute-start(f32[200,128]{1,0:T(8,128)S(1)} %add_add_fusion.1), channel_id=1, source_target_pairs={{0,2},{1,3},{2,0},{3,1},{4,6},{5,7},{6,4},{7,5},{8,10},{9,11},{10,... | collective-permute-start | bytes 307208 | tf_op jit(solution)/shard_map/ppermute | solution.py:292
  150.2 5.7 %collective-permute-start.15 = (f32[200,128]{1,0:T(8,128)S(1)}, f32[200,128]{1,0:T(8,128)S(1)}, u32[]{:S(2)}, u32[]{:S(2)}) collective-permute-start(f32[200,128]{1,0:T(8,128)S(1)} %add_add_fusion.1), channel_id=1, source_target_pairs={{0,1},{1,2},{2,3},{3,0},{4,5},{5,6},{6,7},{7,4},{8,9},{9,10},{10,1... | collective-permute-start | bytes 307208 | tf_op jit(solution)/shard_map/ppermute | solution.py:292

commit v2 on v1

v2 whole, which is shorter than its diff:
```python
import functools
import jax
import jax.numpy as jnp
from jax import lax
from jax.experimental import pallas as pl
from jax.experimental.pallas import tpu as pltpu
from jax.sharding import PartitionSpec as P

L = 64
H = 128
CP = 128
GROUP = 16
WIDE = GROUP * CP
CELLS = 2
DEEP = 4
PAR = 224
HALF = PAR // 2
NT = (((1,), (1,)), ((), ()))
NN = (((1,), (0,)), ((), ()))
F32 = jnp.float32
BF16 = jnp.bfloat16


def dot(a, b, dims=NN):
    return lax.dot_general(a, b, dims, preferred_element_type=F32)


def split(value):
    high = value.astype(BF16)
    return high, (value - high.astype(F32)).astype(BF16)


def put_split(ref, at, value):
    rows = value.shape[0]
    high, low = split(value)
    ref[at:at + rows, :] = high
    ref[at + rows:at + 2 * rows, :] = low


def get_split(ref, at, rows):
    return ref[at:at + rows, :].astype(F32) + ref[at + rows:at + 2 * rows, :].astype(F32)


def column(row, rows):
    return jnp.transpose(jnp.broadcast_to(row, (rows, row.shape[1])))


def pair_kernel(chips, steps, *refs):
    (own_ref, oth_ref), refs = refs[:2], refs[2:]
    row_refs, refs = refs[:2 * chips], refs[2 * chips:]
    col_refs, refs = refs[:2 * steps], refs[2 * steps:]
    (
        w1_ref, b1_ref, ds_ref, w2_ref, b2_ref,
        send_ref, keep_rows, keep_cols, keep_par,
        fixed, even, odd, pos, feat_b, rhs, y_s, slope_s, pm_s, x3_s, env_s, cot_s, split_s,
        racc, cacc, gw2, gds, r_ref, c_ref, par_ref,
    ) = refs
    me_row, me_col = lax.axis_index("row"), lax.axis_index("col")
    me_core = lax.rem(me_col, 2)
    half_rows = chips * CELLS
    half_cols = steps * 2 * CELLS
    for n, ref in enumerate(row_refs):
        r_ref[n * CELLS:(n + 1) * CELLS] = ref[...]
    for n, ref in enumerate(col_refs):
        c_ref[n * 2 * CELLS:(n + 1) * 2 * CELLS] = ref[...]
    slots = (own_ref.shape[0] - 1) // 2
    own_count, oth_count = own_ref[2 * slots], oth_ref[2 * slots]
    both_count = own_count + oth_count
    first_count = jnp.where(me_core == 0, own_count, oth_count)

    def place_row(cell):
        source, inner = cell // CELLS, lax.rem(cell, CELLS)
        step = lax.rem(source // 2 - me_col // 2 + chips, chips)
        return lax.rem(source + me_core, 2) * half_rows + step * CELLS + inner

    def place_col(cell):
        source, inner = cell // CELLS, lax.rem(cell, CELLS)
        step = lax.rem(source // 2 - me_row // 2 + steps, steps)
        return (step * 2 + lax.rem(source + me_row, 2)) * CELLS + inner

    def find(index):
        second = (index >= first_count).astype(jnp.int32)
        entry = index - second * first_count
        mine = second == me_core
        u = jnp.where(mine, own_ref[2 * entry], oth_ref[2 * entry])
        v = jnp.where(mine, own_ref[2 * entry + 1], oth_ref[2 * entry + 1])
        return place_row(u), place_col(v) + jnp.where(mine, 0, half_cols)

    lane = lax.broadcasted_iota(jnp.int32, (H, CP), 1)
    sub = lax.broadcasted_iota(jnp.int32, (8, CP), 0)
    lane2 = lax.broadcasted_iota(jnp.int32, (2 * H, CP), 1)
    zero8 = jnp.zeros((8, CP), F32)
    hot = (
        lax.broadcasted_iota(jnp.int32, (GROUP, WIDE), 1) // CP
        == lax.broadcasted_iota(jnp.int32, (GROUP, WIDE), 0)
    ).astype(F32).astype(BF16)
    for k in range(DEEP):
        rhs[k, 0:GROUP, :] = hot
        rhs[k, GROUP:2 * GROUP, :] = hot
        rhs[k, 2 * GROUP:3 * GROUP, :] = jnp.zeros((GROUP, WIDE), BF16)
    for k in (DEEP - 2, DEEP - 1):
        y_s[k] = jnp.zeros((H, WIDE), BF16)
    x3_s[DEEP - 2] = jnp.zeros((2 * H, WIDE), BF16)
    slope_s[DEEP - 1] = jnp.zeros((H, WIDE), BF16)
    pm_s[DEEP - 1] = jnp.zeros((L, WIDE), F32)
    env_s[DEEP - 1] = jnp.zeros((GROUP, CP), F32)
    cot_s[DEEP - 1] = jnp.zeros((L, CP), F32)
    racc[...] = jnp.zeros_like(racc)
    cacc[...] = jnp.zeros_like(cacc)
    gw2[...] = jnp.zeros_like(gw2)
    gds[...] = jnp.zeros_like(gds)
    b1_b = column(b1_ref[...], CP)
    ds_b = 0.5 * column(ds_ref[...], CP)
    b2_b = 0.5 * jnp.transpose(jnp.broadcast_to(b2_ref[...], (CP, 2 * L)))[:L, :]
    ds_hi = ds_b.astype(BF16).astype(F32)
    ds_lo = ds_b - ds_hi
    w1 = w1_ref[...]
    w1r = w1[:, :L]
    w1f = 0.5 * w1.astype(F32)
    w1f = pltpu.roll(w1f, L, 1)
    fixed[...] = jnp.where(
        lane < L, w1f, jnp.where(lane < 98, ds_hi, jnp.where(lane < 99, ds_lo, 0.0))
    )
    w2f = 0.5 * w2_ref[...].astype(F32)
    w2h = w2f.astype(BF16)
    w2t = jnp.transpose(w2f).astype(BF16)

    def forward_start(k, g):
        first = pl.multiple_of(g * GROUP, GROUP)
        rows = pl.ds(first, GROUP)
        sq = jnp.zeros((GROUP, CP), F32)
        for d in range(3):
            off = pos[d, rows, :] - pos[4, d:d + 1, :]
            sq = sq + off * off
        env_s[k] = pos[3, rows, :] * pos[4, 3:4, :] / ((1.0 + sq) * CP)
        sq_hi = sq.astype(BF16).astype(F32)
        split_s[k, 0:GROUP, :] = sq_hi
        split_s[k, GROUP:2 * GROUP, :] = sq - sq_hi
        for i in range(GROUP):
            at = slice(i * CP, (i + 1) * CP)
            hi_b = jnp.broadcast_to(split_s[k, i:i + 1, :], (8, CP))
            lo_b = jnp.broadcast_to(split_s[k, GROUP + i:GROUP + i + 1, :], (8, CP))
            top = jnp.where(sub == 1, lo_b, jnp.where(sub < 3, hi_b, 0.0))
            rhs[k, 2 * GROUP:3 * GROUP, at] = jnp.concatenate([top, zero8], axis=0).astype(BF16)
        part = pltpu.roll((even if k % 2 == 0 else odd)[...], lax.rem(L - first + CP, CP), 1)
        mix = jnp.where((lane >= L) & (lane < 96), part, fixed[...]).astype(BF16)
        cot_s[k] = pltpu.roll(cot_s[DEEP], lax.rem(CP - first, CP), 1)
        return dot(mix[:, :112], jnp.concatenate([feat_b[...], rhs[k]], axis=0))

    def forward_hidden(k, z):
        for i in range(GROUP):
            at = slice(i * CP, (i + 1) * CP)
            w = z[:, at]
            p = 1.0 + jnp.tanh(w)
            y = (w * p).astype(BF16)
            y_s[k, :, at] = y
            p = p.astype(BF16)
            slope_s[k, :, at] = p + y * (2.0 - p)
        pm_s[k] = dot(w2h, y_s[k])

    def back_message(k):
        for i in range(GROUP):
            at = slice(i * CP, (i + 1) * CP)
            w = pm_s[k, :, at] + b2_b
            t = jnp.tanh(w)
            p = 1.0 + t
            y = w * p
            e = env_s[k, i:i + 1, :]
            x3_s[k, L:2 * L, at] = (y * e).astype(BF16)
            x3_s[k, 0:L, at] = ((p + y - y * t) * (cot_s[k, :, i:i + 1] * e)).astype(BF16)
        return dot(w2t, x3_s[k, 0:L, :])

    def back_hidden(k, gh, v):
        total = cacc[v]
        for i in range(GROUP):
            at = slice(i * CP, (i + 1) * CP)
            inner = gh[:, at].astype(BF16) * slope_s[k, :, at]
            x3_s[k, 2 * L:, at] = inner
            total = total + inner.astype(F32)
        cacc[v] = total

    def back_sums(k, g, u):
        first = pl.multiple_of(g * GROUP, GROUP)
        both = jnp.concatenate([y_s[k], rhs[k, GROUP:3 * GROUP]], axis=0)
        s = dot(x3_s[k], both, NT)
        gw2[...] += s[:L, :H]
        sums = jnp.concatenate([s[:, H:], jnp.zeros((2 * H, CP - 2 * GROUP), F32)], axis=1)
        gds[...] += sums[2 * L:]
        here = (lane2 >= first) & (lane2 < first + GROUP)
        racc[u] += jnp.where(here, pltpu.roll(sums, first, 1), 0.0)

    def half(k, g, v, g_sums, u_sums):
        back = (k - 1) % DEEP
        z = forward_start(k, g)
        back_sums((k - 2) % DEEP, g_sums, u_sums)
        gh = back_message(back)
        forward_hidden(k, z)
        back_hidden(back, gh, v)

    def begin(u, v):
        a = 0.5 * (dot(w1r, r_ref[u, 0:L, :]) + b1_b)
        a_hi = a.astype(BF16).astype(F32)
        a_lo = pltpu.roll(a - a_hi, GROUP, 1)
        block = (lane // GROUP) % 2 == 0
        even[...] = jnp.where(block, a_hi, a_lo)
        odd[...] = jnp.where(block, a_lo, a_hi)
        cot_s[DEEP] = 0.5 * r_ref[u, L:2 * L, :].astype(F32)
        xu = r_ref[u, 2 * L:2 * L + 16, :].astype(F32)
        for d in range(4):
            pos[d] = column(xu[d:d + 1, :], CP)
        pos[4, 0:16, :] = c_ref[v, L:L + 16, :].astype(F32)
        fv = c_ref[v, 0:L, :]
        for i in range(GROUP):
            feat_b[:, i * CP:(i + 1) * CP] = fv

    parts = CP // GROUP // DEEP
    begins = jnp.where(me_core == 0, 0, both_count * parts // 2)
    ends = jnp.where(me_core == 0, both_count * parts // 2, both_count * parts)

    def unit(index, before):
        u_last, v_last, g_last = before
        u, v = find(index // parts)
        g = lax.rem(index, parts) * DEEP

        @pl.when((g == 0) | (index == begins))
        def _():
            begin(u, v)

        for k in range(DEEP):
            g_sums = g + k - 2 if k >= 2 else g_last + DEEP + k - 2
            half(k, g + k, v if k else v_last, g_sums, u if k >= 2 else u_last)
        return u, v, g

    zero = jnp.int32(0)
    u, v, g = lax.fori_loop(begins, ends, unit, (zero, zero, zero))
    gh = back_message(DEEP - 1)
    back_sums(DEEP - 2, g + DEEP - 2, u)
    back_hidden(DEEP - 1, gh, v)
    back_sums(DEEP - 1, g + DEEP - 1, u)

    w1t = 2.0 * jnp.transpose(w1f)
    ones = jnp.ones((GROUP, 8 * CP), BF16)
    par_ref[2 * L:3 * L, :] = gw2[...]
    par_ref[3 * L:, :] = jnp.zeros((PAR - 3 * L, H), F32)
    picked = ((lane >= GROUP) & (lane < GROUP + 2))[:GROUP].astype(F32).astype(BF16)
    high, low = split(gds[...])
    par_ref[3 * L + 1:3 * L + 2, :] = (dot(picked, high, NT) + dot(picked, low, NT))[0:1]

    def block(acc, src, w, start, count, put):
        cells = [start + n for n in range(count)]
        grads = jnp.concatenate([acc[c, acc.shape[1] - H:, :] for c in cells], axis=1)
        feats = jnp.concatenate([src[c, 0:L, :] for c in cells], axis=1)
        high, low = split(grads)
        values = dot(w, high) + dot(w, low)
        left = jnp.concatenate([feats, ones[:, :count * CP]], axis=0)
        for n, c in enumerate(cells):
            put(c, values[:, n * CP:(n + 1) * CP])
        return dot(left, high, NT) + dot(left, low, NT)

    def keep_row(c, value):
        keep_rows[c, 0:L, :] = racc[c, L:2 * L, :]
        keep_rows[c, L:2 * L, :] = value

    def send_row(c, value):
        at = pl.multiple_of((c - half_rows) * 2 * L, 2 * L)
        send_ref[pl.ds(at, L), :] = racc[c, L:2 * L, :].astype(BF16)
        send_ref[pl.ds(at + L, L), :] = value.astype(BF16)

    def keep_col(c, value):
        keep_cols[c] = value

    def send_col(c, value):
        at = pl.multiple_of(half_rows * 2 * L + (c - half_cols) * L, L)
        send_ref[pl.ds(at, L), :] = value.astype(BF16)

    def sweep(acc, src, w, start, total, count, put):
        return lax.fori_loop(
            0, total // count,
            lambda n, part: part + block(acc, src, w, start + n * count, count, put),
            jnp.zeros((L + GROUP, H), F32),
        )

    w_row, w_col = w1t[L:].astype(BF16), w1t[:L].astype(BF16)
    first = sweep(racc, r_ref, w_row, 0, half_rows, 4, keep_row)
    first = first + sweep(racc, r_ref, w_row, half_rows, half_rows, 4, send_row)
    par_ref[0:L, :] = first[:L]
    par_ref[3 * L:3 * L + 1, :] = first[L:L + 1]
    bias2 = jnp.zeros((2 * L, CP), F32)
    for c in range(2 * half_rows):
        bias2 = bias2 + racc[c, :2 * L, :]
    high, low = split(bias2)
    one = ones[:, :CP]
    par_ref[3 * L + 2:3 * L + 3, :] = (dot(one, high, NT) + dot(one, low, NT))[0:1]
    first = sweep(cacc, c_ref, w_col, 0, half_cols, 8, keep_col)
    first = first + sweep(cacc, c_ref, w_col, half_cols, half_cols, 8, send_col)
    par_ref[L:2 * L, :] = first[:L]
    keep_par[...] = par_ref[pl.ds(pl.multiple_of(me_core * HALF, HALF), HALF), :]
    put_split(send_ref, half_rows * 2 * L + half_cols * L,
              par_ref[pl.ds(pl.multiple_of((1 - me_core) * HALF, HALF), HALF), :])


VM = pl.BlockSpec(memory_space=pltpu.VMEM)
SM = pl.BlockSpec(memory_space=pltpu.SMEM)


def call(kernel, name, ins, outs, scratch=(), smem=0, limit=48):
    return pl.pallas_call(
        kernel,
        out_shape=tuple(jax.ShapeDtypeStruct(s, d) for s, d in outs),
        in_specs=[SM] * smem + [VM] * (len(ins) - smem),
        out_specs=(VM,) * len(outs),
        scratch_shapes=list(scratch),
        compiler_params=pltpu.CompilerParams(vmem_limit_bytes=limit * 1024 * 1024),
        name=name,
    )(*ins)


def pair_call(lists, rows, cols, weights):
    chips, steps = len(rows) // 2, len(cols) // 2
    n_row, n_col = 2 * chips * CELLS, 4 * steps * CELLS
    sent = n_row // 2 * 2 * L + n_col // 2 * L + PAR
    return call(
        functools.partial(pair_kernel, chips, steps),
        "pair_tiles",
        [*lists, *rows, *cols, *weights],
        [
            ((sent, CP), BF16),
            ((n_row // 2, 2 * L, CP), F32),
            ((n_col // 2, L, CP), F32),
            ((HALF, H), F32),
        ],
        [
            pltpu.VMEM((H, CP), F32),
            pltpu.VMEM((H, CP), F32),
            pltpu.VMEM((H, CP), F32),
            pltpu.VMEM((5, CP, CP), F32),
            pltpu.VMEM((L, WIDE), BF16),
            pltpu.VMEM((DEEP, 3 * GROUP, WIDE), BF16),
            pltpu.VMEM((DEEP, H, WIDE), BF16),
            pltpu.VMEM((DEEP, H, WIDE), BF16),
            pltpu.VMEM((DEEP, L, WIDE), F32),
            pltpu.VMEM((DEEP, 2 * H, WIDE), BF16),
            pltpu.VMEM((DEEP, GROUP, CP), F32),
            pltpu.VMEM((DEEP + 1, L, CP), F32),
            pltpu.VMEM((DEEP, 2 * GROUP, CP), F32),
            pltpu.VMEM((n_row, 2 * H, CP), F32),
            pltpu.VMEM((n_col, H, CP), F32),
            pltpu.VMEM((L, H), F32),
            pltpu.VMEM((H, CP), F32),
            pltpu.VMEM((n_row,) + rows[0].shape[1:], BF16),
            pltpu.VMEM((n_col,) + cols[0].shape[1:], BF16),
            pltpu.VMEM((PAR, H), F32),
        ],
        smem=2,
    )


def core_sum(chips, steps, recv, rows, cols, par, *outs):
    x_msgs, (y_msg, xy_msg, rows_out, cols_out, par_out) = outs[:chips - 1], outs[chips - 1:]
    n_row, n_col = rows.shape[0], cols.shape[0]
    total = par[...] + get_split(recv, n_row * 2 * L + n_col * L, HALF)
    par_out[...] = total
    put_split(xy_msg, 0, total)
    for c in range(n_row):
        value = rows[c] + recv[c * 2 * L:(c + 1) * 2 * L, :].astype(F32)
        step, inner = c // CELLS, c % CELLS
        if step == 0:
            rows_out[inner] = value
        else:
            x_msgs[step - 1][inner * 2 * L:(inner + 1) * 2 * L, :] = value.astype(BF16)
    for x_msg in x_msgs:
        put_split(x_msg, CELLS * 2 * L, total)
    for c in range(n_col):
        at = n_row * 2 * L + c * L
        value = cols[c] + recv[at:at + L, :].astype(F32)
        slot, inner = c // CELLS, c % CELLS
        to = (slot // 2) * CELLS + inner
        if slot % 2 == 0:
            cols_out[to] = value
        else:
            y_msg[to * L:(to + 1) * L, :] = value.astype(BF16)
    put_split(y_msg, steps * CELLS * L, total)


def near_sum(chips, steps, *refs):
    x_in, refs = refs[:chips - 1], refs[chips - 1:]
    xy_in, refs = refs[:chips - 1], refs[chips - 1:]
    (y_in, rows, cols, par), refs = refs[:4], refs[4:]
    rows_out, cols_out, par_out = refs[:3]
    z_msgs = refs[3:]
    total = par[...] + get_split(y_in, steps * CELLS * L, HALF)
    for ref in x_in:
        total = total + get_split(ref, CELLS * 2 * L, HALF)
    for ref in xy_in:
        total = total + get_split(ref, 0, HALF)
    par_out[...] = total
    for c in range(CELLS):
        value = rows[c]
        for ref in x_in:
            value = value + ref[c * 2 * L:(c + 1) * 2 * L, :].astype(F32)
        rows_out[c] = value
    for c in range(steps * CELLS):
        value = cols[c] + y_in[c * L:(c + 1) * L, :].astype(F32)
        step, inner = c // CELLS, c % CELLS
        if step == 0:
            cols_out[inner] = value
        else:
            z_msgs[step - 1][inner * L:(inner + 1) * L, :] = value.astype(BF16)
    for ref in z_msgs:
        put_split(ref, CELLS * L, total)


def far_sum(steps, *refs):
    z_in, refs = refs[:steps - 1], refs[steps - 1:]
    rows, cols, par, feats, cotangent, updated, grad_feats, par_out = refs
    total = par[...]
    for ref in z_in:
        total = total + get_split(ref, CELLS * L, HALF)
    par_out[...] = total
    for c in range(CELLS):
        value = cols[c]
        for ref in z_in:
            value = value + ref[c * L:(c + 1) * L, :].astype(F32)
        updated[c] = (feats[c].astype(F32) + rows[c, :L, :]).astype(BF16)
        grad_feats[c] = cotangent[c].astype(F32) + rows[c, L:, :] + value


def gather_halves(own, oth, first, bias1, dist, second, bias2, par):
    core = lax.rem(lax.axis_index("col"), 2)
    par[pl.ds(pl.multiple_of(core * HALF, HALF), HALF), :] = own[...]
    par[pl.ds(pl.multiple_of((1 - core) * HALF, HALF), HALF), :] = oth[...]
    first[...] = jnp.transpose(par[:2 * L, :])
    second[...] = par[2 * L:3 * L, :]
    bias1[...] = par[3 * L:3 * L + 1, :]
    dist[...] = par[3 * L + 1:3 * L + 2, :]
    bias2[...] = par[3 * L + 2:3 * L + 3, :]


def per_device(
    feats, coords, valid, pairs, pair_count, w_first, bias_first, dist_scale,
    w_second, bias_second, cotangent, rows_n, cols_n,
):
    steps, chips = rows_n // 2, cols_n // 2
    swap_y = [(i, i ^ 1) for i in range(rows_n)]
    swap_core = [(i, i ^ 1) for i in range(cols_n)]

    def along(n, d):
        return [(i, (i + 2 * d) % n) for i in range(n)]

    def diagonal(d):
        return [
            (r * cols_n + c, (r ^ 1) * cols_n + (c + 2 * d) % cols_n)
            for r in range(rows_n) for c in range(cols_n)
        ]

    extra = jnp.concatenate(
        [coords, valid.astype(BF16)[:, None], jnp.zeros((CELLS, 12, CP), BF16)], axis=1
    )
    col_own = jnp.concatenate([feats, extra], axis=1)
    row_own = jnp.concatenate([feats, cotangent, extra], axis=1)
    tiles = jnp.concatenate([pairs.reshape(-1), pair_count.reshape(-1)])
    col_pair = jnp.concatenate([col_own, lax.ppermute(col_own, "row", swap_y)], axis=0)
    row_parts = [row_own] + [
        lax.ppermute(row_own, "col", along(cols_n, -d)) for d in range(1, chips)
    ]
    col_parts = [col_pair] + [
        lax.ppermute(col_pair, "row", along(rows_n, -d)) for d in range(1, steps)
    ]
    other_tiles = lax.ppermute(tiles, "col", swap_core)
    row_parts += [lax.ppermute(p, "col", swap_core) for p in row_parts]
    col_parts += [lax.ppermute(p, "col", swap_core) for p in col_parts]
    send, rows, cols, par = pair_call(
        [tiles, other_tiles], row_parts, col_parts,
        [
            w_first, bias_first.reshape(1, H), dist_scale.reshape(1, H), w_second,
            jnp.pad(bias_second, (0, L)).reshape(1, 2 * L),
        ],
    )
    got = lax.ppermute(send, "col", swap_core)
    x_shape = ((CELLS * 2 * L + PAR, CP), BF16)
    keep = [((CELLS, 2 * L, CP), F32), ((steps * CELLS, L, CP), F32), ((HALF, H), F32)]
    outs = call(
        functools.partial(core_sum, chips, steps), "core_sum", [got, rows, cols, par],
        [x_shape] * (chips - 1)
        + [((steps * CELLS * L + PAR, CP), BF16), ((PAR, H), BF16)] + keep,
    )
    x_msgs, (y_msg, xy_msg, rows, cols, par) = outs[:chips - 1], outs[chips - 1:]
    y_in = lax.ppermute(y_msg, "row", swap_y)
    x_in = [lax.ppermute(m, "col", along(cols_n, d + 1)) for d, m in enumerate(x_msgs)]
    xy_in = [lax.ppermute(xy_msg, ("row", "col"), diagonal(d)) for d in range(1, chips)]
    keep[1] = ((CELLS, L, CP), F32)
    rows, cols, par, *z_msgs = call(
        functools.partial(near_sum, chips, steps), "near_sum",
        [*x_in, *xy_in, y_in, rows, cols, par],
        keep + [((CELLS * L + PAR, CP), BF16)] * (steps - 1),
    )
    z_in = [lax.ppermute(m, "row", along(rows_n, d + 1)) for d, m in enumerate(z_msgs)]
    updated, grad_feats, par = call(
        functools.partial(far_sum, steps), "far_sum",
        [*z_in, rows, cols, par, feats, cotangent],
        [((CELLS, L, CP), BF16), ((CELLS, L, CP), F32), ((HALF, H), F32)],
    )
    first, bias1, dist, second, bias2 = call(
        gather_halves, "gather_halves", [par, lax.ppermute(par, "col", swap_core)],
        [((H, 2 * L), F32), ((1, H), F32), ((1, H), F32), ((L, H), F32), ((1, H), F32)],
        [pltpu.VMEM((PAR, H), F32)],
    )
    return updated, grad_feats, first, bias1[0], dist[0], second, bias2[0, :L]


def solution(mesh):
    spread = P(("row", "col"))
    placed = (spread, spread, spread, P("row", "col"), P("row", "col"), P(), P(), P(), P(), P(), spread)
    return jax.shard_map(
        functools.partial(per_device, rows_n=mesh.shape["row"], cols_n=mesh.shape["col"]),
        mesh=mesh,
        in_specs=placed,
        out_specs=(spread, spread, P(), P(), P(), P(), P()),
        check_vma=False,
    )
```

time: 160 us -> 93.5 us (0.58)
  starting transfers between devices: 108 us -> 40.9 us
  Pallas kernels: 20.3 us -> 32 us
  blocking collectives: 5.92 us -> 0 us
  local copies, waits for them, and re-layouts: 4.15 us -> 1.56 us
    ppermute x18 -> x20, starting transfers between devices: 108 us -> 40.9 us  [the longest x3 24.7 us: per_device(): lax.ppermute(m, 'row', along(rows_n, d + 1))]
    pallas_call x1 -> x5, Pallas kernels: 20.3 us -> 32 us  [call(): pl.pallas_call(kernel, out_shape=tuple((jax.ShapeDtypeStruct(s, d) for s,...]
    all_gather x1 -> x0, blocking collectives: 5.92 us -> none  [per_device(): row_pack = lax.all_gather(row_own, 'col', axis=0, tiled=True)]
    ppermute x18 -> x20, waiting for transfers between devices: 15.7 us -> 14.9 us  [the longest x1 4.61 us: per_device(): lax.ppermute(xy_msg, ('row', 'col'), diagonal(d))]
  transfers between devices with their start and end apart: 18 -> 20, of which waited for: 4 -> 13; matrix products, arithmetic and copies ran while one was open for 1% -> 0% of each run, Pallas kernels for 0% -> 0%
where the time goes in v2:
time: 93.5 us; the launch traced here: 92.3 us
  starting transfers between devices  40.9 us (44%)
  Pallas kernels  32 us (34%)
  waiting for transfers between devices  14.9 us (16%)
  other arithmetic  1.61 us (2%)
  local copies, waits for them, and re-layouts  1.56 us (2%)
  between operations  1.42 us (2%)
    pallas_call x5, Pallas kernels, call(): pl.pallas_call(kernel, out_shape=tuple((jax.ShapeDtypeStruct(s, d) for s,...  32 us
    ppermute x3, starting transfers between devices, per_device(): lax.ppermute(m, 'row', along(rows_n, d + 1))  24.7 us
    ppermute x3, starting transfers between devices, per_device(): lax.ppermute(col_pair, 'row', along(rows_n, -d))  6.07 us
    ppermute x1, waiting for transfers between devices, per_device(): lax.ppermute(xy_msg, ('row', 'col'), diagonal(d))  4.61 us
    ppermute x1, starting transfers between devices, per_device(): lax.ppermute(xy_msg, ('row', 'col'), diagonal(d))  3.41 us
    ppermute x1, starting transfers between devices, per_device(): lax.ppermute(col_own, 'row', swap_y)  3.03 us
    ppermute x1, waiting for transfers between devices, per_device(): lax.ppermute(row_own, 'col', along(cols_n, -d))  2.88 us
    ppermute x3, waiting for transfers between devices, per_device(): lax.ppermute(m, 'row', along(rows_n, d + 1))  2.14 us
  transfers between devices with their start and end apart: 20, of which 13 were waited for; matrix products, arithmetic and copies ran while one was open for 0% of the time, Pallas kernels for 0%

profile of v2, /device:TPU:0, one launch (start us, length us, event | category | flops | bytes accessed | tf_op | source)
XLA Modules:
  0.0 92.3 jit_solution(5296003205396097206)
XLA Ops:
  0.6 0.7 convert_bitcast_fusion
  1.4 0.0 copy-start
  1.4 0.8 pad_maximum_fusion.1
  2.2 0.0 copy-start.7
  2.2 3.0 %collective-permute-start.4 = (bf16[2,80,128]{2,1,0:T(8,128)(2,1)S(1)}, bf16[2,80,128]{2,1,0:T(8,128)(2,1)S(1)}, u32[]{:S(2)}, u32[]{:S(2)}) collective-permute-start(bf16[2,80,128]{2,1,0:T(8,128)(2,1)S(1)} %pad_maximum_fusion.1), channel_id=1, source_target_pairs={{0,4},{4,0},{8,12},{12,8},{16,20},{20,16},{24,28},{28,24},{1,5},{5... | collective-permute-start | bytes 122888 | tf_op jit(solution)/shard_map/ppermute | solution.py:462
  5.9 0.1 copy.21
  6.0 0.1 reshape.29
  6.1 1.2 %collective-permute-done.4 = bf16[2,80,128]{2,1,0:T(8,128)(2,1)S(1)} collective-permute-done((bf16[2,80,128]{2,1,0:T(8,128)(2,1)S(1)}, bf16[2,80,128]{2,1,0:T(8,128)(2,1)S(1)}, u32[]{:S(2)}, u32[]{:S(2)}) %collective-permute-start.4) | collective-permute-done | bytes 40992 | tf_op jit(solution)/shard_map/ppermute | solution.py:462
  7.3 2.1 %collective-permute-start.7 = (bf16[4,80,128]{2,1,0:T(8,128)(2,1)S(1)}, bf16[4,80,128]{2,1,0:T(8,128)(2,1)S(1)}, u32[]{:S(2)}, u32[]{:S(2)}) collective-permute-start(bf16[4,80,128]{2,1,0:T(8,128)(2,1)S(1)} %pad_maximum_fusion.refs_6_), channel_id=1, source_target_pairs={{0,8},{4,12},{8,16},{12,20},{16,24},{20,28},{24,0},{28,4},{1,9},{5... | collective-permute-start | bytes 245768 | tf_op jit(solution)/shard_map/ppermute | solution.py:467
  9.4 2.6 %collective-permute-start.6 = (bf16[4,80,128]{2,1,0:T(8,128)(2,1)S(1)}, bf16[4,80,128]{2,1,0:T(8,128)(2,1)S(1)}, u32[]{:S(2)}, u32[]{:S(2)}) collective-permute-start(bf16[4,80,128]{2,1,0:T(8,128)(2,1)S(1)} %pad_maximum_fusion.refs_6_), channel_id=1, source_target_pairs={{0,16},{4,20},{8,24},{12,28},{16,0},{20,4},{24,8},{28,12},{1,17},{... | collective-permute-start | bytes 245768 | tf_op jit(solution)/shard_map/ppermute | solution.py:467
  12.0 1.3 %collective-permute-start.5 = (bf16[4,80,128]{2,1,0:T(8,128)(2,1)S(1)}, bf16[4,80,128]{2,1,0:T(8,128)(2,1)S(1)}, u32[]{:S(2)}, u32[]{:S(2)}) collective-permute-start(bf16[4,80,128]{2,1,0:T(8,128)(2,1)S(1)} %pad_maximum_fusion.refs_6_), channel_id=1, source_target_pairs={{0,24},{4,28},{8,0},{12,4},{16,8},{20,12},{24,16},{28,20},{1,25},{... | collective-permute-start | bytes 245768 | tf_op jit(solution)/shard_map/ppermute | solution.py:467
  13.3 0.1 pad_add_fusion.refs_0_
  13.4 0.0 collective-permute-start
  13.4 0.0 copy-start.3
  13.4 0.2 concatenate.16.refs_2_
  13.6 0.5 collective-permute-start.2
  14.2 0.4 collective-permute-done.refs_1_
  14.5 1.5 %collective-permute-start.1 = (bf16[2,144,128]{2,1,0:T(8,128)(2,1)S(1)}, bf16[2,144,128]{2,1,0:T(8,128)(2,1)S(1)}, u32[]{:S(2)}, u32[]{:S(2)}) collective-permute-start(bf16[2,144,128]{2,1,0:T(8,128)(2,1)S(1)} %concatenate.16.refs_2_), channel_id=1, source_target_pairs={{0,2},{1,3},{2,0},{3,1},{4,6},{5,7},{6,4},{7,5},{8,10},{9,11},{10,... | collective-permute-start | bytes 221192 | tf_op jit(solution)/shard_map/ppermute | solution.py:464
  16.0 0.0 collective-permute-done.2.refs_4_
  16.0 2.9 %collective-permute-done.1.refs_3_ = bf16[2,144,128]{2,1,0:T(8,128)(2,1)S(1)} collective-permute-done((bf16[2,144,128]{2,1,0:T(8,128)(2,1)S(1)}, bf16[2,144,128]{2,1,0:T(8,128)(2,1)S(1)}, u32[]{:S(2)}, u32[]{:S(2)}) %collective-permute-start.1) | collective-permute-done | bytes 73760 | tf_op jit(solution)/shard_map/ppermute | solution.py:464
  18.9 0.5 collective-permute-start.11
  19.4 0.1 collective-permute-start.10
  19.5 0.4 collective-permute-start.9
  20.0 0.2 collective-permute-done.3.refs_5_
  20.2 0.2 collective-permute-done.11.refs_13_
  20.4 0.4 collective-permute-done.10.refs_12_
  20.7 0.2 collective-permute-done.9.refs_11_
  20.9 0.6 copy-done.4
  21.5 0.0 copy-done.5
  21.5 30.4 %pair_tiles.1 = (bf16[1760,128]{1,0:T(8,128)(2,1)S(1)}, f32[4,128,128]{2,1,0:T(8,128)S(1)}, f32[16,64,128]{2,1,0:T(8,128)S(1)}, f32[112,128]{1,0:T(8,128)S(1)}) custom-call(s32[17]{0:T(128)S(1)} %pad_add_fusion.refs_0_, s32[17]{0:T(128)S(1)} %collective-permute-done.refs_1_, bf16[2,144,128]{2,1,0:T(8,128)(2,1)S(1)} %concatenate.16.refs_2_, ...), custom_call_target="tpu_custom_call" | custom-call | tf_op jit(solution)/shard_map/pair_tiles/pallas_call | solution.py:307
  52.0 0.4 collective-permute-start.12
  52.4 1.4 %collective-permute-done.12.recv = bf16[1760,128]{1,0:T(8,128)(2,1)S(1)} collective-permute-done((bf16[1760,128]{1,0:T(8,128)(2,1)S(1)}, bf16[1760,128]{1,0:T(8,128)(2,1)S(1)}, u32[]{:S(2)}, u32[]{:S(2)}) %collective-permute-start.12) | collective-permute-done | bytes 450592 | tf_op jit(solution)/shard_map/ppermute | solution.py:479
  53.9 0.1 core_sum.1
  54.0 0.1 collective-permute-start.15
  54.0 0.1 collective-permute-start.13
  54.1 3.4 %collective-permute-start.14 = (bf16[224,128]{1,0:T(8,128)(2,1)S(1)}, bf16[224,128]{1,0:T(8,128)(2,1)S(1)}, u32[]{:S(2)}, u32[]{:S(2)}) collective-permute-start(bf16[224,128]{1,0:T(8,128)(2,1)S(1)} %get-tuple-element.36), channel_id=1, source_target_pairs={{0,6},{1,7},{2,4},{3,5},{4,2},{5,3},{6,0},{7,1},{8,14},{9,15},{10,... | collective-permute-start | bytes 172040 | tf_op jit(solution)/shard_map/ppermute | solution.py:490
  57.5 4.6 %collective-permute-done.14.refs_1_ = bf16[224,128]{1,0:T(8,128)(2,1)S(1)} collective-permute-done((bf16[224,128]{1,0:T(8,128)(2,1)S(1)}, bf16[224,128]{1,0:T(8,128)(2,1)S(1)}, u32[]{:S(2)}, u32[]{:S(2)}) %collective-permute-start.14) | collective-permute-done | bytes 57376 | tf_op jit(solution)/shard_map/ppermute | solution.py:490
  62.1 0.1 collective-permute-done.15.refs_2_
  62.3 0.1 near_sum.1
  62.3 0.7 collective-permute-start.16
  63.1 21.1 %collective-permute-start.17 = (bf16[352,128]{1,0:T(8,128)(2,1)S(1)}, bf16[352,128]{1,0:T(8,128)(2,1)S(1)}, u32[]{:S(2)}, u32[]{:S(2)}) collective-permute-start(bf16[352,128]{1,0:T(8,128)(2,1)S(1)} %get-tuple-element.42), channel_id=1, source_target_pairs={{0,16},{4,20},{8,24},{12,28},{16,0},{20,4},{24,8},{28,12},{1,17},{... | collective-permute-start | bytes 270344 | tf_op jit(solution)/shard_map/ppermute | solution.py:497
  84.2 2.8 %collective-permute-start.18 = (bf16[352,128]{1,0:T(8,128)(2,1)S(1)}, bf16[352,128]{1,0:T(8,128)(2,1)S(1)}, u32[]{:S(2)}, u32[]{:S(2)}) collective-permute-start(bf16[352,128]{1,0:T(8,128)(2,1)S(1)} %get-tuple-element.43), channel_id=1, source_target_pairs={{0,24},{4,28},{8,0},{12,4},{16,8},{20,12},{24,16},{28,20},{1,25},{... | collective-permute-start | bytes 270344 | tf_op jit(solution)/shard_map/ppermute | solution.py:497
  87.0 1.4 %collective-permute-done.17.refs_1_ = bf16[352,128]{1,0:T(8,128)(2,1)S(1)} collective-permute-done((bf16[352,128]{1,0:T(8,128)(2,1)S(1)}, bf16[352,128]{1,0:T(8,128)(2,1)S(1)}, u32[]{:S(2)}, u32[]{:S(2)}) %collective-permute-start.17) | collective-permute-done | bytes 90144 | tf_op jit(solution)/shard_map/ppermute | solution.py:497
  88.4 0.8 collective-permute-done.18.refs_2_
  89.2 0.7 far_sum.1
  89.8 1.2 %collective-permute-done.19.oth = f32[112,128]{1,0:T(8,128)S(1)} collective-permute-done((f32[112,128]{1,0:T(8,128)S(1)}, f32[112,128]{1,0:T(8,128)S(1)}, u32[]{:S(2)}, u32[]{:S(2)}) %collective-permute-start.19) | collective-permute-done | bytes 57376 | tf_op jit(solution)/shard_map/ppermute | solution.py:504
  91.1 0.8 gather_halves.1
  91.8 0.5 slice_bitcast_fusion
  (27 shorter events, 0.1 us)
Async XLA Ops:
  0.6 0.7 copy-start.6
  1.4 5.9 %copy-start = (bf16[2,64,128]{2,1,0:T(8,128)(2,1)S(1)}, bf16[2,64,128]{2,1,0:T(8,128)(2,1)}, u32[]{:S(2)}) copy-start(bf16[2,64,128]{2,1,0:T(8,128)(2,1)} %refs_6_.1) | copy-start | bytes 98308
  2.2 3.7 %copy-start.7 = (s32[1,1,8,2]{2,3,1,0:T(2,128)S(1)}, s32[1,1,8,2]{2,3,1,0:T(2,128)}, u32[]{:S(2)}) copy-start(s32[1,1,8,2]{2,3,1,0:T(2,128)} %param.14) | copy-start | bytes 196
  2.2 5.0 %collective-permute-start.4 = (bf16[2,80,128]{2,1,0:T(8,128)(2,1)S(1)}, bf16[2,80,128]{2,1,0:T(8,128)(2,1)S(1)}, u32[]{:S(2)}, u32[]{:S(2)}) collective-permute-start(bf16[2,80,128]{2,1,0:T(8,128)(2,1)S(1)} %pad_maximum_fusion.1), channel_id=1, source_target_pairs={{0,4},{4,0},{8,12},{12,8},{16,20},{20,16},{24,28},{28,24},{1,5},{5... | collective-permute-start | bytes 122888 | tf_op jit(solution)/shard_map/ppermute | solution.py:462
  6.1 7.4 %copy-start.1 = (bf16[2,64,128]{2,1,0:T(8,128)(2,1)S(1)}, bf16[2,64,128]{2,1,0:T(8,128)(2,1)}, u32[]{:S(2)}) copy-start(bf16[2,64,128]{2,1,0:T(8,128)(2,1)} %refs_7_.1) | copy-start | bytes 98308
  7.3 11.7 %collective-permute-start.7 = (bf16[4,80,128]{2,1,0:T(8,128)(2,1)S(1)}, bf16[4,80,128]{2,1,0:T(8,128)(2,1)S(1)}, u32[]{:S(2)}, u32[]{:S(2)}) collective-permute-start(bf16[4,80,128]{2,1,0:T(8,128)(2,1)S(1)} %pad_maximum_fusion.refs_6_), channel_id=1, source_target_pairs={{0,8},{4,12},{8,16},{12,20},{16,24},{20,28},{24,0},{28,4},{1,9},{5... | collective-permute-start | bytes 245768 | tf_op jit(solution)/shard_map/ppermute | solution.py:467
  9.4 10.1 %collective-permute-start.6 = (bf16[4,80,128]{2,1,0:T(8,128)(2,1)S(1)}, bf16[4,80,128]{2,1,0:T(8,128)(2,1)S(1)}, u32[]{:S(2)}, u32[]{:S(2)}) collective-permute-start(bf16[4,80,128]{2,1,0:T(8,128)(2,1)S(1)} %pad_maximum_fusion.refs_6_), channel_id=1, source_target_pairs={{0,16},{4,20},{8,24},{12,28},{16,0},{20,4},{24,8},{28,12},{1,17},{... | collective-permute-start | bytes 245768 | tf_op jit(solution)/shard_map/ppermute | solution.py:467
  12.0 7.5 %collective-permute-start.5 = (bf16[4,80,128]{2,1,0:T(8,128)(2,1)S(1)}, bf16[4,80,128]{2,1,0:T(8,128)(2,1)S(1)}, u32[]{:S(2)}, u32[]{:S(2)}) collective-permute-start(bf16[4,80,128]{2,1,0:T(8,128)(2,1)S(1)} %pad_maximum_fusion.refs_6_), channel_id=1, source_target_pairs={{0,24},{4,28},{8,0},{12,4},{16,8},{20,12},{24,16},{28,20},{1,25},{... | collective-permute-start | bytes 245768 | tf_op jit(solution)/shard_map/ppermute | solution.py:467
  13.4 6.6 %copy-start.8 = (f32[64]{0:T(128)S(1)}, f32[64]{0:T(128)}, u32[]{:S(2)}) copy-start(f32[64]{0:T(128)} %param.20) | copy-start | bytes 772
  13.4 7.5 %copy-start.2 = (bf16[128,128]{1,0:T(8,128)(2,1)S(1)}, bf16[128,128]{1,0:T(8,128)(2,1)}, u32[]{:S(2)}) copy-start(bf16[128,128]{1,0:T(8,128)(2,1)} %refs_14_.1) | copy-start | bytes 98308
  13.4 1.1 %collective-permute-start = (s32[17]{0:T(128)S(1)}, s32[17]{0:T(128)S(1)}, u32[]{:S(2)}, u32[]{:S(2)}) collective-permute-start(s32[17]{0:T(128)S(1)} %pad_add_fusion.refs_0_), channel_id=1, source_target_pairs={{0,1},{1,0},{2,3},{3,2},{4,5},{5,4},{6,7},{7,6},{8,9},{9,8},{10,11... | collective-permute-start | bytes 212 | tf_op jit(solution)/shard_map/ppermute | solution.py:469
  13.4 7.4 %copy-start.3 = (bf16[64,128]{1,0:T(8,128)(2,1)S(1)}, bf16[64,128]{1,0:T(8,128)(2,1)}, u32[]{:S(2)}) copy-start(bf16[64,128]{1,0:T(8,128)(2,1)} %refs_17_.1) | copy-start | bytes 49156
  13.6 2.4 %collective-permute-start.2 = (bf16[2,144,128]{2,1,0:T(8,128)(2,1)S(1)}, bf16[2,144,128]{2,1,0:T(8,128)(2,1)S(1)}, u32[]{:S(2)}, u32[]{:S(2)}) collective-permute-start(bf16[2,144,128]{2,1,0:T(8,128)(2,1)S(1)} %concatenate.16.refs_2_), channel_id=1, source_target_pairs={{0,1},{1,0},{2,3},{3,2},{4,5},{5,4},{6,7},{7,6},{8,9},{9,8},{10,11... | collective-permute-start | bytes 221192 | tf_op jit(solution)/shard_map/ppermute | solution.py:470
  14.5 4.4 %collective-permute-start.1 = (bf16[2,144,128]{2,1,0:T(8,128)(2,1)S(1)}, bf16[2,144,128]{2,1,0:T(8,128)(2,1)S(1)}, u32[]{:S(2)}, u32[]{:S(2)}) collective-permute-start(bf16[2,144,128]{2,1,0:T(8,128)(2,1)S(1)} %concatenate.16.refs_2_), channel_id=1, source_target_pairs={{0,2},{1,3},{2,0},{3,1},{4,6},{5,7},{6,4},{7,5},{8,10},{9,11},{10,... | collective-permute-start | bytes 221192 | tf_op jit(solution)/shard_map/ppermute | solution.py:464
  16.0 3.9 %collective-permute-start.8 = (bf16[4,80,128]{2,1,0:T(8,128)(2,1)S(1)}, bf16[4,80,128]{2,1,0:T(8,128)(2,1)S(1)}, u32[]{:S(2)}, u32[]{:S(2)}) collective-permute-start(bf16[4,80,128]{2,1,0:T(8,128)(2,1)S(1)} %pad_maximum_fusion.refs_6_), channel_id=1, source_target_pairs={{0,1},{1,0},{2,3},{3,2},{4,5},{5,4},{6,7},{7,6},{8,9},{9,8},{10,11... | collective-permute-start | bytes 245768 | tf_op jit(solution)/shard_map/ppermute | solution.py:471
  18.9 1.3 %collective-permute-start.3 = (bf16[2,144,128]{2,1,0:T(8,128)(2,1)S(1)}, bf16[2,144,128]{2,1,0:T(8,128)(2,1)S(1)}, u32[]{:S(2)}, u32[]{:S(2)}) collective-permute-start(bf16[2,144,128]{2,1,0:T(8,128)(2,1)S(1)} %collective-permute-done.1.refs_3_), channel_id=1, source_target_pairs={{0,1},{1,0},{2,3},{3,2},{4,5},{5,4},{6,7},{7,6},{8,9},{9,8},{10,11... | collective-permute-start | bytes 221192 | tf_op jit(solution)/shard_map/ppermute | solution.py:470
  18.9 1.4 %collective-permute-start.11 = (bf16[4,80,128]{2,1,0:T(8,128)(2,1)S(1)}, bf16[4,80,128]{2,1,0:T(8,128)(2,1)S(1)}, u32[]{:S(2)}, u32[]{:S(2)}) collective-permute-start(bf16[4,80,128]{2,1,0:T(8,128)(2,1)S(1)} %collective-permute-done.7.refs_9_), channel_id=1, source_target_pairs={{0,1},{1,0},{2,3},{3,2},{4,5},{5,4},{6,7},{7,6},{8,9},{9,8},{10,11... | collective-permute-start | bytes 245768 | tf_op jit(solution)/shard_map/ppermute | solution.py:471
  19.4 1.3 %collective-permute-start.10 = (bf16[4,80,128]{2,1,0:T(8,128)(2,1)S(1)}, bf16[4,80,128]{2,1,0:T(8,128)(2,1)S(1)}, u32[]{:S(2)}, u32[]{:S(2)}) collective-permute-start(bf16[4,80,128]{2,1,0:T(8,128)(2,1)S(1)} %collective-permute-done.6.refs_8_), channel_id=1, source_target_pairs={{0,1},{1,0},{2,3},{3,2},{4,5},{5,4},{6,7},{7,6},{8,9},{9,8},{10,11... | collective-permute-start | bytes 245768 | tf_op jit(solution)/shard_map/ppermute | solution.py:471
  19.5 1.4 %collective-permute-start.9 = (bf16[4,80,128]{2,1,0:T(8,128)(2,1)S(1)}, bf16[4,80,128]{2,1,0:T(8,128)(2,1)S(1)}, u32[]{:S(2)}, u32[]{:S(2)}) collective-permute-start(bf16[4,80,128]{2,1,0:T(8,128)(2,1)S(1)} %collective-permute-done.5.refs_7_), channel_id=1, source_target_pairs={{0,1},{1,0},{2,3},{3,2},{4,5},{5,4},{6,7},{7,6},{8,9},{9,8},{10,11... | collective-permute-start | bytes 245768 | tf_op jit(solution)/shard_map/ppermute | solution.py:471
  20.9 0.7 copy-start.4
  20.9 0.7 copy-start.5
  52.0 1.9 %collective-permute-start.12 = (bf16[1760,128]{1,0:T(8,128)(2,1)S(1)}, bf16[1760,128]{1,0:T(8,128)(2,1)S(1)}, u32[]{:S(2)}, u32[]{:S(2)}) collective-permute-start(bf16[1760,128]{1,0:T(8,128)(2,1)S(1)} %get-tuple-element.31), channel_id=1, source_target_pairs={{0,1},{1,0},{2,3},{3,2},{4,5},{5,4},{6,7},{7,6},{8,9},{9,8},{10,11... | collective-permute-start | bytes 1351688 | tf_op jit(solution)/shard_map/ppermute | solution.py:479
  54.0 8.3 %collective-permute-start.15 = (bf16[736,128]{1,0:T(8,128)(2,1)S(1)}, bf16[736,128]{1,0:T(8,128)(2,1)S(1)}, u32[]{:S(2)}, u32[]{:S(2)}) collective-permute-start(bf16[736,128]{1,0:T(8,128)(2,1)S(1)} %get-tuple-element.37), channel_id=1, source_target_pairs={{0,4},{4,0},{8,12},{12,8},{16,20},{20,16},{24,28},{28,24},{1,5},{5... | collective-permute-start | bytes 565256 | tf_op jit(solution)/shard_map/ppermute | solution.py:488
  54.0 8.1 %collective-permute-start.13 = (bf16[480,128]{1,0:T(8,128)(2,1)S(1)}, bf16[480,128]{1,0:T(8,128)(2,1)S(1)}, u32[]{:S(2)}, u32[]{:S(2)}) collective-permute-start(bf16[480,128]{1,0:T(8,128)(2,1)S(1)} %get-tuple-element.35), channel_id=1, source_target_pairs={{0,2},{1,3},{2,0},{3,1},{4,6},{5,7},{6,4},{7,5},{8,10},{9,11},{10,... | collective-permute-start | bytes 368648 | tf_op jit(solution)/shard_map/ppermute | solution.py:489
  54.1 8.0 %collective-permute-start.14 = (bf16[224,128]{1,0:T(8,128)(2,1)S(1)}, bf16[224,128]{1,0:T(8,128)(2,1)S(1)}, u32[]{:S(2)}, u32[]{:S(2)}) collective-permute-start(bf16[224,128]{1,0:T(8,128)(2,1)S(1)} %get-tuple-element.36), channel_id=1, source_target_pairs={{0,6},{1,7},{2,4},{3,5},{4,2},{5,3},{6,0},{7,1},{8,14},{9,15},{10,... | collective-permute-start | bytes 172040 | tf_op jit(solution)/shard_map/ppermute | solution.py:490
  62.3 24.7 %collective-permute-start.16 = (bf16[352,128]{1,0:T(8,128)(2,1)S(1)}, bf16[352,128]{1,0:T(8,128)(2,1)S(1)}, u32[]{:S(2)}, u32[]{:S(2)}) collective-permute-start(bf16[352,128]{1,0:T(8,128)(2,1)S(1)} %get-tuple-element.41), channel_id=1, source_target_pairs={{0,8},{4,12},{8,16},{12,20},{16,24},{20,28},{24,0},{28,4},{1,9},{5... | collective-permute-start | bytes 270344 | tf_op jit(solution)/shard_map/ppermute | solution.py:497
  63.1 25.3 %collective-permute-start.17 = (bf16[352,128]{1,0:T(8,128)(2,1)S(1)}, bf16[352,128]{1,0:T(8,128)(2,1)S(1)}, u32[]{:S(2)}, u32[]{:S(2)}) collective-permute-start(bf16[352,128]{1,0:T(8,128)(2,1)S(1)} %get-tuple-element.42), channel_id=1, source_target_pairs={{0,16},{4,20},{8,24},{12,28},{16,0},{20,4},{24,8},{28,12},{1,17},{... | collective-permute-start | bytes 270344 | tf_op jit(solution)/shard_map/ppermute | solution.py:497
  84.2 5.0 %collective-permute-start.18 = (bf16[352,128]{1,0:T(8,128)(2,1)S(1)}, bf16[352,128]{1,0:T(8,128)(2,1)S(1)}, u32[]{:S(2)}, u32[]{:S(2)}) collective-permute-start(bf16[352,128]{1,0:T(8,128)(2,1)S(1)} %get-tuple-element.43), channel_id=1, source_target_pairs={{0,24},{4,28},{8,0},{12,4},{16,8},{20,12},{24,16},{28,20},{1,25},{... | collective-permute-start | bytes 270344 | tf_op jit(solution)/shard_map/ppermute | solution.py:497
  89.8 1.2 %collective-permute-start.19 = (f32[112,128]{1,0:T(8,128)S(1)}, f32[112,128]{1,0:T(8,128)S(1)}, u32[]{:S(2)}, u32[]{:S(2)}) collective-permute-start(f32[112,128]{1,0:T(8,128)S(1)} %get-tuple-element.49.own), channel_id=1, source_target_pairs={{0,1},{1,0},{2,3},{3,2},{4,5},{5,4},{6,7},{7,6},{8,9},{9,8},{10,11... | collective-permute-start | bytes 172040 | tf_op jit(solution)/shard_map/ppermute | solution.py:504
